TPU v7x, 256 devices: a whole 4x4x8 slice. The times are simulated.
256 devices in a mesh: dp: 4 (over x_lo, core), seq: 16 (over x_hi, z), tensor: 4 (over y).
Axes of the slice: x: 4 (x_hi: 2, x_lo: 2; x = x_hi * 2 + x_lo), y: 4, z: 8, core: 2. Of those that a mesh axis runs over, the one named last changes fastest.
Arguments:
- tokens: bfloat16 [12288, 4096], P(('dp', 'seq'), 'tensor'), parts along dimension 0, may hold values from -40 to 40
- input_projection_weight: bfloat16 [4096, 3072], P(None, 'tensor'), may hold values from -0.09375 to 0.09375
- w_out: bfloat16 [2048, 4096], P('tensor'), may hold values from -0.125 to 0.125
- upstream: bfloat16 [12288, 4096], P(('dp', 'seq'), 'tensor'), parts along dimension 0, may hold values from -6 to 6
- exponents: int32 [768, 24], P('dp', 'tensor'), parts along dimension 0, may hold values from -7 to -1
Outputs:
- attended: bfloat16 [12288, 4096], P(('dp', 'seq'), 'tensor'), parts along dimension 0
- grad_tokens: bfloat16 [12288, 4096], P(('dp', 'seq'), 'tensor'), parts along dimension 0
- grad_w_qkv: bfloat16 [16384, 3072], P(('dp', 'seq'), 'tensor'), parts along dimension 0
- grad_w_out: bfloat16 [8192, 4096], P(('dp', 'tensor'), 'seq'), parts along dimension 0
There are 4 independent parts, one for each index of `dp`. A program takes and returns all parts, laid end to end along the dimension named above; an argument that names none is the same for every part. Nothing has to cross between parts.
All inputs are finite; a program needn't handle non-finite values.
Results may differ from a plain program's by a relative error of at most 0.029.
The roundings to bfloat16 on the way count: a program that leaves them out, or rounds other values in their place, can miss the bound.
Values may be sent and summed in bfloat16 or wider, within the bound.
A program may use at most 128 MiB of HBM per device.

v0:
```python
import math

import jax
import jax.numpy as jnp
from jax import lax
from jax.sharding import PartitionSpec as P

HEAD_SIZE = 128
QUERY_PER_KEY = 4
SCALE_TOKENS = 16


THETA = 500000.0


def rotate(vectors, places, sign):
    half = vectors.shape[-1] // 2
    freqs = jnp.power(
        jnp.float32(THETA), -jnp.arange(half, dtype=jnp.float32) * 2.0 / vectors.shape[-1]
    )
    angles = places.astype(jnp.float32)[:, None] * freqs[None, :]
    cosine = jnp.cos(angles)[:, None, :]
    sine = sign * jnp.sin(angles)[:, None, :]
    first = vectors[..., :half]
    second = vectors[..., half:]
    return jnp.concatenate(
        [first * cosine - second * sine, second * cosine + first * sine], axis=-1
    )


def dot_rows(left, right):
    return lax.dot_general(
        left, right, (((1,), (1,)), ((), ())), preferred_element_type=jnp.float32
    )


def dot_cols(left, right):
    return lax.dot_general(
        left, right, (((0,), (0,)), ((), ())), preferred_element_type=jnp.float32
    )


def forward_block(query, query_places, keys, values, key_places):
    scale = 1.0 / math.sqrt(query.shape[-1])
    scores = dot_rows(query, keys) * scale
    allowed = key_places[None, :] <= query_places[:, None]
    scores = jnp.where(allowed, scores, -jnp.inf)
    top = jnp.max(scores, axis=1, keepdims=True)
    weights = jnp.exp(scores - top)
    total = jnp.sum(weights, axis=1, keepdims=True)
    mixed = (
        jnp.dot(weights.astype(jnp.bfloat16), values, preferred_element_type=jnp.float32) / total
    )
    return (mixed.astype(jnp.bfloat16), (top + jnp.log(total))[:, 0])


def backward_block(query, query_places, grad_out, output, logsum, keys, values, key_places):
    scale = 1.0 / math.sqrt(query.shape[-1])
    scores = dot_rows(query, keys) * scale
    allowed = key_places[None, :] <= query_places[:, None]
    probs = jnp.exp(jnp.where(allowed, scores - logsum[:, None], -jnp.inf))
    grad_values = dot_cols(probs.astype(jnp.bfloat16), grad_out)
    grad_probs = dot_rows(grad_out, values)
    delta = jnp.sum(
        grad_out.astype(jnp.float32) * output.astype(jnp.float32), axis=1, keepdims=True
    )
    grad_scores = (probs * (grad_probs - delta)).astype(jnp.bfloat16)
    grad_query = jnp.dot(grad_scores, keys, preferred_element_type=jnp.float32) * scale
    grad_keys = dot_cols(grad_scores, query) * scale
    return (grad_query, grad_keys, grad_values)


def squeeze(gradient, scale_exponent):
    scaled = jnp.clip(gradient * jnp.exp2(-scale_exponent)[..., None], -127.0, 127.0)
    sent = lax.optimization_barrier(scaled.astype(jnp.bfloat16))
    return sent.astype(jnp.float32) * jnp.exp2(scale_exponent)[..., None]


def to_heads(array, pieces):
    rows, head_layout, model_width = array.shape
    sub_rows = rows // pieces
    return (
        array.reshape(pieces, sub_rows, head_layout, model_width)
        .transpose(2, 0, 1, 3)
        .reshape(head_layout * pieces, sub_rows, model_width)
    )


def from_heads(array, pieces):
    number, sub_rows, model_width = array.shape
    head_layout = number // pieces
    return (
        array.reshape(head_layout, pieces, sub_rows, model_width)
        .transpose(1, 2, 0, 3)
        .reshape(pieces * sub_rows, head_layout, model_width)
    )


def local(tokens, input_projection_weight, w_out, upstream, exponents):
    rows = tokens.shape[0]
    seq_count = lax.axis_size("seq")
    seq_index = lax.axis_index("seq")
    head_dim = HEAD_SIZE
    kv_local = input_projection_weight.shape[1] // (6 * head_dim)
    heads_local = QUERY_PER_KEY * kv_local
    pieces = max(1, seq_count // heads_local)
    sub_rows = rows // pieces
    items = heads_local * pieces // seq_count
    query_rows = seq_count * sub_rows
    total_rows = rows * seq_count
    block = math.gcd(query_rows, 512)
    places = seq_index * rows + jnp.arange(rows, dtype=jnp.int32)
    key_places = jnp.arange(total_rows, dtype=jnp.int32)
    weight_rows = input_projection_weight
    projected_rows = jnp.dot(
        lax.all_gather(tokens, "tensor", axis=1, tiled=True),
        weight_rows,
        preferred_element_type=jnp.float32,
    )
    projected_rows = projected_rows.reshape(rows, kv_local, 6, head_dim)
    query = rotate(
        projected_rows[:, :, :QUERY_PER_KEY].reshape(rows, heads_local, head_dim), places, 1.0
    ).astype(jnp.bfloat16)
    keys = rotate(projected_rows[:, :, QUERY_PER_KEY], places, 1.0).astype(jnp.bfloat16)
    values = projected_rows[:, :, QUERY_PER_KEY + 1].astype(jnp.bfloat16)
    query_heads = lax.all_to_all(
        to_heads(query, pieces), "seq", split_axis=0, concat_axis=1, tiled=True
    )
    keys_all, values_all = (
        lax.all_gather(keys, "seq", axis=0, tiled=True),
        lax.all_gather(values, "seq", axis=0, tiled=True),
    )
    item_ids = seq_index * items + jnp.arange(items, dtype=jnp.int32)
    head_ids = item_ids // pieces
    piece_ids = item_ids % pieces
    kv_ids = head_ids // QUERY_PER_KEY
    sources = jnp.arange(seq_count, dtype=jnp.int32)
    within = jnp.arange(sub_rows, dtype=jnp.int32)
    query_places = (
        sources[None, :, None] * rows + piece_ids[:, None, None] * sub_rows + within[None, None, :]
    ).reshape(items, query_rows)

    def item_forward(packed):
        query_item, place_item, kv_id = packed
        key_item = lax.dynamic_index_in_dim(keys_all, kv_id, 1, keepdims=False)
        value_item = lax.dynamic_index_in_dim(values_all, kv_id, 1, keepdims=False)
        return lax.map(
            lambda blocks: forward_block(blocks[0], blocks[1], key_item, value_item, key_places),
            (query_item.reshape(-1, block, head_dim), place_item.reshape(-1, block)),
        )

    out_blocks, logsum_blocks = lax.map(item_forward, (query_heads, query_places, kv_ids))
    out_heads = out_blocks.reshape(items, query_rows, head_dim)
    logsum_heads = logsum_blocks.reshape(items, query_rows)
    out_tokens = from_heads(
        lax.all_to_all(out_heads, "seq", split_axis=1, concat_axis=0, tiled=True), pieces
    ).reshape(rows, heads_local * head_dim)
    columns = w_out
    attended = (
        lax.psum_scatter(
            dot_cols(columns, out_tokens.T).astype(jnp.bfloat16),
            "tensor",
            scatter_dimension=0,
            tiled=True,
        )
        .astype(jnp.float32)
        .T.astype(jnp.bfloat16)
    )
    piece = lax.all_gather(upstream, "tensor", axis=1, tiled=True)
    columns = w_out
    grad_acc = dot_rows(piece, columns)
    weight_acc = dot_cols(out_tokens, piece)
    grad_w_out = lax.psum_scatter(
        weight_acc.astype(jnp.bfloat16), "seq", scatter_dimension=1, tiled=True
    )
    grad_heads = lax.all_to_all(
        to_heads(grad_acc.astype(jnp.bfloat16).reshape(rows, heads_local, head_dim), pieces),
        "seq",
        split_axis=0,
        concat_axis=1,
        tiled=True,
    )
    expo_heads = exponents.astype(jnp.float32).reshape(
        seq_count, pieces, sub_rows // SCALE_TOKENS, kv_local * 6
    )

    def item_backward(packed):
        query_item, place_item, kv_id, head_id, piece_id, grad_item, out_item, logsum_item = packed
        key_item = lax.dynamic_index_in_dim(keys_all, kv_id, 1, keepdims=False)
        value_item = lax.dynamic_index_in_dim(values_all, kv_id, 1, keepdims=False)

        def step(carry, blocks):
            grad_query, key_gradient, value_gradient = backward_block(
                blocks[0],
                blocks[1],
                blocks[2],
                blocks[3],
                blocks[4],
                key_item,
                value_item,
                key_places,
            )
            return ((carry[0] + key_gradient, carry[1] + value_gradient), grad_query)

        zeros = jnp.zeros((total_rows, head_dim), jnp.float32)
        sums, grad_query = lax.scan(
            step,
            (zeros, zeros),
            (
                query_item.reshape(-1, block, head_dim),
                place_item.reshape(-1, block),
                grad_item.reshape(-1, block, head_dim),
                out_item.reshape(-1, block, head_dim),
                logsum_item.reshape(-1, block),
            ),
        )
        column = kv_id * 6 + head_id % QUERY_PER_KEY
        scales = lax.dynamic_index_in_dim(
            lax.dynamic_index_in_dim(expo_heads, piece_id, 1, keepdims=False),
            column,
            2,
            keepdims=False,
        )
        scales = jnp.broadcast_to(
            scales[:, :, None], (seq_count, sub_rows // SCALE_TOKENS, SCALE_TOKENS)
        ).reshape(query_rows)
        wire = jnp.clip(
            grad_query.reshape(query_rows, head_dim) * jnp.exp2(-scales)[:, None], -127.0, 127.0
        ).astype(jnp.bfloat16)
        return (wire, sums[0], sums[1])

    wire_heads, key_terms, value_terms = lax.map(
        item_backward,
        (
            query_heads,
            query_places,
            kv_ids,
            head_ids,
            piece_ids,
            grad_heads,
            out_heads,
            logsum_heads,
        ),
    )
    selector = (kv_ids[:, None] == jnp.arange(kv_local, dtype=jnp.int32)[None, :]).astype(
        jnp.float32
    )
    key_sum = jnp.einsum("itd,ik->tkd", key_terms, selector, precision=lax.Precision.HIGHEST)
    value_sum = jnp.einsum("itd,ik->tkd", value_terms, selector, precision=lax.Precision.HIGHEST)
    key_rows_gradient, value_rows_gradient = (
        lax.psum_scatter(key_sum, "seq", scatter_dimension=0, tiled=True),
        lax.psum_scatter(value_sum, "seq", scatter_dimension=0, tiled=True),
    )
    mine = lax.dynamic_slice_in_dim(
        exponents, seq_index * (rows // SCALE_TOKENS), rows // SCALE_TOKENS, 0
    ).astype(jnp.float32)
    mine = jnp.repeat(mine, SCALE_TOKENS, axis=0).reshape(rows, kv_local, 6)
    query_back = from_heads(
        lax.all_to_all(wire_heads, "seq", split_axis=1, concat_axis=0, tiled=True), pieces
    )
    query_gradient = (
        query_back.astype(jnp.float32)
        * jnp.exp2(mine[:, :, :QUERY_PER_KEY].reshape(rows, heads_local))[:, :, None]
    )
    query_gradient = rotate(query_gradient, places, -1.0).astype(jnp.bfloat16)
    key_rows_gradient = rotate(
        squeeze(key_rows_gradient, mine[:, :, QUERY_PER_KEY]), places, -1.0
    ).astype(jnp.bfloat16)
    value_rows_gradient = squeeze(value_rows_gradient, mine[:, :, QUERY_PER_KEY + 1]).astype(
        jnp.bfloat16
    )
    projection_gradient = jnp.concatenate(
        [
            query_gradient.reshape(rows, kv_local, QUERY_PER_KEY, head_dim),
            key_rows_gradient[:, :, None],
            value_rows_gradient[:, :, None],
        ],
        axis=2,
    ).reshape(rows, kv_local * 6 * head_dim)
    weight_rows = input_projection_weight
    grad_tokens = (
        lax.psum_scatter(
            dot_rows(weight_rows, projection_gradient).astype(jnp.bfloat16),
            "tensor",
            scatter_dimension=0,
            tiled=True,
        )
        .astype(jnp.float32)
        .T.astype(jnp.bfloat16)
    )
    gathered = lax.all_gather(tokens, "tensor", axis=1, tiled=True)
    grad_w_qkv = lax.psum_scatter(
        dot_cols(gathered, projection_gradient).astype(jnp.bfloat16),
        "seq",
        scatter_dimension=0,
        tiled=True,
    )
    return (attended, grad_tokens, grad_w_qkv, grad_w_out)


def solution(mesh):
    in_specs = (
        P(("dp", "seq"), "tensor"),
        P(None, "tensor"),
        P("tensor", None),
        P(("dp", "seq"), "tensor"),
        P("dp", "tensor"),
    )
    out_specs = (
        P(("dp", "seq"), "tensor"),
        P(("dp", "seq"), "tensor"),
        P(("dp", "seq"), "tensor"),
        P(("dp", "tensor"), "seq"),
    )
    return jax.shard_map(local, mesh=mesh, in_specs=in_specs, out_specs=out_specs, check_vma=False)
```

profile of v0, /device:TPU:2, one launch (start us, length us, event | category | flops | bytes accessed | tf_op | source)
XLA Modules:
  0.0 1137.6 jit_solution(1992534233348024858)
XLA Ops:
  10.1 31.8 %all-gather.4.cloned.1.call-done = bf16[192,4096]{1,0:T(8,128)(2,1)} async-done(((bf16[192,1024]{1,0:T(8,128)(2,1)}), bf16[192,4096]{1,0:T(8,128)(2,1)}) %all-gather.4.cloned.1.call-update) | async-done | bytes 1572880 | tf_op jit(solution)/shard_map/all_gather | solution.py:116
  41.9 4.7 fusion.84
  48.3 8.7 all-to-all-start
  57.5 47.7 %all_gather.14 = bf16[3072,1,128]{2,0,1:T(8,128)(2,1)} all-gather(bf16[192,1,128]{2,0,1:T(8,128)(2,1)S(1)} %pad_maximum_fusion.2), channel_id=1, replica_groups=mesh['dp'=4,'seq'=16,'tensor'=4] {'seq'}, dimensions={0}, use_global_device_ids=true | all-gather | bytes 835584 | tf_op jit(solution)/shard_map/all_gather | solution.py:130
  105.2 4.2 convolution_convert_fusion.4
  110.2 43.2 %all-gather = bf16[3072,1,1,128]{3,0,2,1:T(8,128)(2,1)} all-gather(bf16[192,1,1,128]{3,0,2,1:T(8,128)(2,1)S(1)} %copy.66), channel_id=2, replica_groups=mesh['dp'=4,'seq'=16,'tensor'=4] {'seq'}, dimensions={0}, use_global_device_ids=true | all-gather | bytes 835584 | tf_op jit(solution)/shard_map/all_gather | solution.py:131
  153.4 3.7 all-to-all-start.2
  157.2 16.9 %while.48 = (s32[]{:T(128)}, bf16[3,256,128]{2,1,0:T(8,128)(2,1)S(1)}, f32[3,256]{1,0:T(4,128)}, s32[3,256]{1,0:T(4,128)S(1)}, bf16[3,256,128]{2,1,0:T(8,128)(2,...) while((s32[]{:T(128)}, ...), condition=%wide.region_3.4_spmd.clone, body=%wide.region_0.3_spmd.clone.sunk | while | flops 409009920 | bytes 11155049 | solution.py:147
  157.2 1.9 fusion.124
  159.7 1.3 dynamic_update_slice.35
  161.0 1.8 fusion.126
  162.8 1.9 fusion.124
  166.6 1.8 fusion.126
  168.5 1.9 fusion.124
  172.2 1.8 fusion.126
  174.1 36.8 %while.49 = (s32[]{:T(128)}, f32[3072,128]{1,0:T(8,128)}, f32[3072,128]{1,0:T(8,128)}, f32[3,256,128]{2,1,0:T(8,128)}, s32[3,256]{1,0:T(4,128)S(1)}, /*index=5*/...) while((s32[]{:T(128)}, f32[3072,128]{1,0:T(8,128)}, ...), condition=%wide.region_7.8_spmd.clone, body=%wide.region_5.7_spmd.clone.sunk | while | flops 1015054080 | bytes 67381056 | solution.py:206
  174.8 2.2 fusion.137
  177.1 1.5 copy-done
  180.0 2.2 fusion.140
  183.5 1.9 convolution_add_fusion.2
  186.1 2.2 fusion.137
  188.4 1.5 copy-done
  191.3 2.2 fusion.140
  194.8 3.3 convolution_add_fusion.2
  198.8 2.2 fusion.137
  201.1 1.5 copy-done
  204.0 2.2 fusion.140
  207.5 3.3 convolution_add_fusion.2
  210.8 2.7 multiply_bitcast_fusion.1
  213.8 2.7 multiply_bitcast_fusion
  218.0 2.2 fusion.83
  220.8 1.8 reduce.1
  223.3 9.6 all-to-all-start.3
  233.2 10.0 all-to-all-done.3
  244.7 174.8 %reduce-scatter.9.cloned.1.call-done = f32[192,1,128]{2,0,1:T(8,128)} async-done(((f32[3072,1,128]{2,0,1:T(8,128)}), f32[192,1,128]{2,0,1:T(8,128)}) %reduce-scatter.9.cloned.1.call-update) | async-done | bytes 98320 | tf_op jit(solution)/shard_map/reduce_scatter | solution.py:251
  421.2 206.0 %reduce-scatter.11.cloned.1.call-done = f32[192,1,128]{2,0,1:T(8,128)} async-done(((f32[3072,1,128]{2,0,1:T(8,128)}), f32[192,1,128]{2,0,1:T(8,128)}) %reduce-scatter.11.cloned.1.call-update) | async-done | bytes 98320 | tf_op jit(solution)/shard_map/reduce_scatter | solution.py:252
  628.9 4.5 fusion.47
  633.8 1.8 reduce
  635.7 17.9 %all_to_all.16 = bf16[16,2,3072]{2,1,0:T(2,128)(2,1)S(1)} all-to-all(bf16[16,2,3072]{2,1,0:T(2,128)(2,1)S(1)} %reshape.553), channel_id=1, replica_groups=mesh['dp'=4,'seq'=16,'tensor'=4] {'seq'}, dimensions={0} | all-to-all | bytes 393216 | tf_op jit(solution)/shard_map/all_to_all | solution.py:156
  653.9 4.3 fusion.48
  658.3 6.3 fusion.49
  664.7 1.3 copy-done.7
  666.0 3.4 convolution_convert_fusion.1
  669.4 182.9 %reduce-scatter.15.cloned.1.call-done = bf16[256,768]{0,1:T(8,128)(2,1)} async-done(((bf16[4096,768]{0,1:T(8,128)(2,1)}), bf16[256,768]{0,1:T(8,128)(2,1)}) %reduce-scatter.15.cloned.1.call-update) | async-done | bytes 393232 | tf_op jit(solution)/shard_map/reduce_scatter | solution.py:292
  852.3 1.9 copy.77
  854.2 28.8 %reduce-scatter.7.cloned.1.call-done = bf16[1024,192]{0,1:T(8,128)(2,1)} async-done(((bf16[4096,192]{0,1:T(8,128)(2,1)}), bf16[1024,192]{0,1:T(8,128)(2,1)}) %reduce-scatter.7.cloned.1.call-update) | async-done | bytes 393232 | tf_op jit(solution)/shard_map/reduce_scatter | solution.py:160
  883.0 31.4 %reduce-scatter.13.cloned.1.call-done = bf16[1024,192]{0,1:T(8,128)(2,1)} async-done(((bf16[4096,192]{0,1:T(8,128)(2,1)}), bf16[1024,192]{0,1:T(8,128)(2,1)}) %reduce-scatter.13.cloned.1.call-update) | async-done | bytes 393232 | tf_op jit(solution)/shard_map/reduce_scatter | solution.py:282
  914.4 216.3 %reduce-scatter.17.cloned.1.call-done = bf16[512,256]{1,0:T(8,128)(2,1)} async-done(((bf16[512,4096]{1,0:T(8,128)(2,1)}), bf16[512,256]{1,0:T(8,128)(2,1)}) %reduce-scatter.17.cloned.1.call-update) | async-done | bytes 262160 | tf_op jit(solution)/shard_map/reduce_scatter | solution.py:173
  (162 shorter events, 29.3 us)
Async XLA Ops:
  7.2 34.7 %all-gather.4.cloned.1.call-start = ((), (), s32[]{:S(2)}) async-start(), calls=%async_computation.10 | async-start | bytes 1966080 | tf_op jit(solution)/shard_map/all_gather | solution.py:116
  7.9 97.3 %all-gather.6.cloned.1.call-start = ((), (), s32[]{:S(2)}) async-start(), calls=%async_computation.12 | async-start | bytes 1966080 | tf_op jit(solution)/shard_map/all_gather | solution.py:169
  9.0 47.9 %copy-start.15 = (f32[64]{0:T(128)}, f32[64]{0:T(128)S(1)}, u32[]{:S(2)}) copy-start(f32[64]{0:T(128)S(1)} %multiply_power_fusion) | copy-start | bytes 772
  9.0 47.9 %copy-start.13 = (f32[192]{0:T(256)}, f32[192]{0:T(256)S(1)}, u32[]{:S(2)}) copy-start(f32[192]{0:T(256)S(1)} %add_convert_fusion.2) | copy-start | bytes 2308
  10.1 36.8 %copy-start.8 = (f32[192,64]{1,0:T(8,128)}, f32[192,64]{1,0:T(8,128)S(1)}, u32[]{:S(2)}) copy-start(f32[192,64]{1,0:T(8,128)S(1)} %get-tuple-element.321) | copy-start | bytes 147460
  48.3 105.2 %all-to-all-start = ((bf16[16,48,128]{2,1,0:T(8,128)(2,1)}), bf16[16,48,128]{2,1,0:T(8,128)(2,1)}, u32[]{:S(2)}, u32[]{:S(2)}) async-start(bf16[16,48,128]{2,1,0:T(8,128)(2,1)} %bitcast.6), calls=%async_computation | async-start | bytes 393216 | tf_op jit(solution)/shard_map/all_to_all | solution.py:126
  153.4 20.7 %all-to-all-start.2 = ((bf16[16,48,128]{2,1,0:T(8,128)(2,1)}), bf16[16,48,128]{2,1,0:T(8,128)(2,1)S(1)}, u32[]{:S(2)}, u32[]{:S(2)}) async-start(bf16[16,48,128]{2,1,0:T(8,128)(2,1)} %bitcast.16), calls=%async_computation.3 | async-start | bytes 393216 | tf_op jit(solution)/shard_map/all_to_all | solution.py:176
  157.1 262.4 %reduce-scatter.9.cloned.1.call-start = ((), (), s32[]{:S(2)}) async-start(), calls=%async_computation.13 | async-start | bytes 1671168 | tf_op jit(solution)/shard_map/reduce_scatter | solution.py:251
  174.8 3.8 copy-start.2
  176.9 1.6 copy-start
  178.6 1.4 copy-start.3
  180.0 2.3 copy-start.5
  180.0 3.5 copy-start.1
  182.3 3.2 copy-start.4
  186.1 3.8 copy-start.2
  188.3 1.6 copy-start
  189.9 1.4 copy-start.3
  191.3 2.3 copy-start.5
  191.3 3.5 copy-start.1
  193.6 4.6 copy-start.4
  198.8 3.8 copy-start.2
  201.0 1.6 copy-start
  202.6 1.4 copy-start.3
  204.0 2.3 copy-start.5
  204.0 3.5 copy-start.1
  206.3 4.6 copy-start.4
  213.5 413.7 %reduce-scatter.11.cloned.1.call-start = ((), (), s32[]{:S(2)}) async-start(), calls=%async_computation.14 | async-start | bytes 1671168 | tf_op jit(solution)/shard_map/reduce_scatter | solution.py:252
  216.5 0.7 copy-start.12
  216.5 1.6 copy-start.10
  223.3 19.8 %all-to-all-start.3 = ((bf16[16,2,3072]{2,1,0:T(2,128)(2,1)}), bf16[16,2,3072]{2,1,0:T(2,128)(2,1)S(1)}, u32[]{:S(2)}, u32[]{:S(2)}) async-start(bf16[16,2,3072]{2,1,0:T(2,128)(2,1)} %reshape.555), calls=%async_computation.4 | async-start | bytes 393216 | tf_op jit(solution)/shard_map/all_to_all | solution.py:259
  232.9 619.3 %reduce-scatter.15.cloned.1.call-start = ((), (), s32[]{:S(2)}) async-start(), calls=%async_computation.16 | async-start | bytes 6684672 | tf_op jit(solution)/shard_map/reduce_scatter | solution.py:292
  243.3 0.9 copy-start.9
  243.3 0.9 copy-start.11
  243.4 177.2 %copy-start.14 = (f32[192]{0:T(256)S(1)}, f32[192]{0:T(256)}, u32[]{:S(2)}) copy-start(f32[192]{0:T(256)} %copy-done.13) | copy-start | bytes 2308
  243.4 177.2 %copy-start.16 = (f32[64]{0:T(128)S(1)}, f32[64]{0:T(128)}, u32[]{:S(2)}) copy-start(f32[64]{0:T(128)} %copy-done.15) | copy-start | bytes 772
  244.3 384.7 %copy-start.6 = (bf16[192,4096]{1,0:T(8,128)(2,1)S(1)}, bf16[192,4096]{1,0:T(8,128)(2,1)}, u32[]{:S(2)}) copy-start(bf16[192,4096]{1,0:T(8,128)(2,1)} %all-gather.4.cloned.1.call-done) | copy-start | bytes 4718596
  633.5 249.6 %reduce-scatter.7.cloned.1.call-start = ((), (), s32[]{:S(2)}) async-start(), calls=%async_computation.11 | async-start | bytes 1966080 | tf_op jit(solution)/shard_map/reduce_scatter | solution.py:160
  658.3 256.1 %reduce-scatter.13.cloned.1.call-start = ((), (), s32[]{:S(2)}) async-start(), calls=%async_computation.15 | async-start | bytes 1966080 | tf_op jit(solution)/shard_map/reduce_scatter | solution.py:282
  664.6 1.4 copy-start.7
  664.6 466.1 %reduce-scatter.17.cloned.1.call-start = ((), (), s32[]{:S(2)}) async-start(), calls=%async_computation.17 | async-start | bytes 4456448 | tf_op jit(solution)/shard_map/reduce_scatter | solution.py:173
Sparse Core Ops, SparseCore 0:
  9.8 32.0 all-gather.3
  43.7 29.1 all-gather.5
  213.7 205.8 reduce-scatter.8
  423.7 203.4 reduce-scatter.10
  633.6 218.6 reduce-scatter.14
  855.4 27.5 reduce-scatter.6
  886.3 28.0 reduce-scatter.12
  919.5 211.1 reduce-scatter.16
where the time goes:
time: 1140 us
  waiting for transfers between devices  884 us (78%)
  blocking collectives  109 us (10%)
  matrix products  65.7 us (6%)
  starting transfers between devices  22.5 us (2%)
  local copies, waits for them, and re-layouts  21.9 us (2%)
  other arithmetic  20.2 us (2%)
  between operations  14.7 us (1%)
    reduce_scatter x1, waiting for transfers between devices, local(): lax.psum_scatter(weight_acc.astype(jnp.bfloat16), 'seq', scatter_dimensio...  216 us
    reduce_scatter x1, waiting for transfers between devices, local(): lax.psum_scatter(value_sum, 'seq', scatter_dimension=0, tiled=True)  206 us
    reduce_scatter x1, waiting for transfers between devices, local(): lax.psum_scatter(dot_cols(gathered, projection_gradient).astype(jnp.bfloa...  183 us
    reduce_scatter x1, waiting for transfers between devices, local(): lax.psum_scatter(key_sum, 'seq', scatter_dimension=0, tiled=True)  175 us
    all_gather x1, blocking collectives, local(): lax.all_gather(keys, 'seq', axis=0, tiled=True)  47.7 us
    all_gather x1, blocking collectives, local(): lax.all_gather(values, 'seq', axis=0, tiled=True)  43.2 us
    all_gather x1, waiting for transfers between devices, local(): lax.all_gather(tokens, 'tensor', axis=1, tiled=True)  31.8 us
    reduce_scatter x1, waiting for transfers between devices, local(): lax.psum_scatter(dot_rows(weight_rows, projection_gradient).astype(jnp.bf...  31.4 us
  transfers between devices with their start and end apart: 11, of which 8 were waited for; matrix products, arithmetic and copies ran while one was open for 5% of the time, Pallas kernels for 0%

commit v1 on v0

v1 whole, which is shorter than its diff:
```python
import functools
import math

import jax
import jax.numpy as jnp
from jax import lax
from jax.experimental import pallas as pl
from jax.experimental.pallas import tpu as pltpu
from jax.sharding import PartitionSpec as P

HEAD_SIZE = 128
QUERY_PER_KEY = 4
SCALE_TOKENS = 16
THETA = 500000.0

NZ = 8
NT = 4
ROWS = 192
QROWS = QUERY_PER_KEY * ROWS
CHUNK = 256
WIDTH = 1024
MESH = pl.DeviceIdType.MESH
BF16 = jnp.bfloat16
F32 = jnp.float32
SCALE = 1.0 / math.sqrt(HEAD_SIZE)
SCALE2 = SCALE * math.log2(math.e)
VMEM_LIMIT = 60 * 2**20


def dot(left, right, left_dim, right_dim):
    return lax.dot_general(
        left, right, (((left_dim,), (right_dim,)), ((), ())), preferred_element_type=F32
    )


class Place:
    def __init__(self):
        self.d = lax.axis_index("dp")
        self.s = lax.axis_index("seq")
        self.t = lax.axis_index("tensor")
        self.xh = lax.div(self.s, NZ)
        self.z = lax.rem(self.s, NZ)

    def tensor(self, offset):
        return (self.d, self.s, lax.rem(self.t + offset, NT))

    def zdev(self, sign):
        return (self.d, self.xh * NZ + lax.rem(self.z + sign + NZ, NZ), self.t)

    def xdev(self):
        return (self.d, (1 - self.xh) * NZ + self.z, self.t)

    def enter(self):
        barrier = pltpu.get_barrier_semaphore()
        partners = [self.tensor(1), self.tensor(2), self.tensor(3)]
        partners += [self.zdev(1), self.zdev(-1), self.xdev()]
        for partner in partners:
            pl.semaphore_signal(barrier, inc=1, device_id=partner, device_id_type=MESH)
        pl.semaphore_wait(barrier, len(partners))


def remote(src, dst, send_sem, recv_sem, device):
    return pltpu.make_async_remote_copy(
        src_ref=src,
        dst_ref=dst,
        send_sem=send_sem,
        recv_sem=recv_sem,
        device_id=device,
        device_id_type=MESH,
    )


def turn(vectors, cosine, sine):
    return vectors * cosine + pltpu.roll(vectors, HEAD_SIZE // 2, 1) * sine


def gather_column(place, kv, column, which, ss, rs, sends):
    def block(z):
        return kv.at[column * NZ + lax.rem(z + 2 * NZ, NZ)]

    def part(step, di, ref):
        return ref.at[pl.ds(di * ROWS, ROWS)] if step == 4 else ref

    def arrived(step, di, sign):
        ref = part(step, di, block(place.z - sign * step))
        sem = rs.at[which, di, step - 1]
        remote(ref, ref, ss.at[which, di, step - 1], sem, place.zdev(sign)).wait_recv()

    for step in range(1, 5):
        for di, sign in ((0, 1), (1, -1)):
            if step > 1:
                arrived(step - 1, di, sign)
            ref = part(step, di, block(place.z - sign * (step - 1)))
            copy = remote(
                ref,
                ref,
                ss.at[which, di, step - 1],
                rs.at[which, di, step - 1],
                place.zdev(sign),
            )
            copy.start()
            sends.append(copy)
        yield
    for di, sign in ((0, 1), (1, -1)):
        arrived(4, di, sign)


def scatter_ring(place, subs, rows, load, sbuf, rbuf, ss, rs, sends, done):
    half = rows // 2
    for step in (4, 3, 2, 1):
        for sub in range(subs):
            for di, sign in ((0, 1), (1, -1)):
                dest = lax.rem(place.z + sign * step + NZ, NZ)
                cut = pl.ds(di * half, half)
                here = sbuf.at[di, step - 1, sub]
                there = rbuf.at[di, step - 1, sub]
                if step == 4:
                    here, there = here.at[cut], there.at[cut]
                    here[...] = load(dest, sub, di).astype(BF16)
                else:
                    value = load(dest, sub, None)
                    before = rbuf.at[di, step, sub]
                    if step == 3:
                        before = before.at[cut]
                    remote(
                        before, before, ss.at[di, step, sub], rs.at[di, step, sub], place.zdev(sign)
                    ).wait_recv()
                    if step == 3:
                        here[cut] = (value[di * half : (di + 1) * half] + before[...]).astype(BF16)
                        rest = 1 - di
                        here[pl.ds(rest * half, half)] = value[
                            rest * half : (rest + 1) * half
                        ].astype(BF16)
                    else:
                        here[...] = (value + before[...]).astype(BF16)
                copy = remote(
                    here, there, ss.at[di, step - 1, sub], rs.at[di, step - 1, sub], place.zdev(sign)
                )
                copy.start()
                sends.append(copy)
            yield
    for sub in range(subs):
        total = load(place.z, sub, None)
        for di, sign in ((0, 1), (1, -1)):
            ref = rbuf.at[di, 0, sub]
            remote(ref, ref, ss.at[di, 0, sub], rs.at[di, 0, sub], place.zdev(sign)).wait_recv()
            total = total + ref[...]
        done(sub, total)


def run(steps, count=None):
    if count is None:
        for _ in steps:
            pass
    else:
        for _ in range(count):
            next(steps)


def project_kernel(
    tok, up, wq_hbm, wo_hbm, cosine, sine,
    q_out, kv, do_out, tok_all, up_all, tok_other,
    wq, wo, load_sem, tok_ss, tok_rs, up_ss, up_rs, x_ss, x_rs, kv_ss, kv_rs,
):
    place = Place()
    t = place.t
    loads = []
    for i in range(NT):
        rows = pl.ds(pl.multiple_of(lax.rem(t + (0, 1, 3, 2)[i], NT) * WIDTH, WIDTH), WIDTH)
        loads.append(pltpu.make_async_copy(wq_hbm.at[rows], wq.at[rows], load_sem.at[i]))
        loads[-1].start()
    load_wo = pltpu.make_async_copy(wo_hbm, wo, load_sem.at[4])
    load_wo.start()
    place.enter()
    sends = []

    def spread(own, everyone, ss, rs):
        for offset in (1, 3, 2):
            copy = remote(
                own, everyone.at[t], ss.at[offset - 1], rs.at[offset - 1], place.tensor(offset)
            )
            copy.start()
            sends.append(copy)

    def arrived(everyone, offset, ss, rs):
        source = lax.rem(t + NT - offset, NT)
        ref = everyone.at[source]
        remote(ref, ref, ss.at[offset - 1], rs.at[offset - 1], place.tensor(offset)).wait_recv()
        return source

    spread(tok, tok_all, tok_ss, tok_rs)
    tok_all[t] = tok[...]
    up_all[t] = up[...]
    loads[0].wait()
    acc = dot(tok[...], wq[pl.ds(pl.multiple_of(t * WIDTH, WIDTH), WIDTH)], 1, 0)
    for load in loads[1:]:
        load.wait()
    for offset in (1, 3, 2):
        source = arrived(tok_all, offset, tok_ss, tok_rs)
        rows = pl.ds(pl.multiple_of(source * WIDTH, WIDTH), WIDTH)
        if offset == 2:
            for copy in sends:
                copy.wait_send()
            sends.clear()
            spread(up, up_all, up_ss, up_rs)
        acc = acc + dot(tok_all[source], wq[rows], 1, 0)

    c, s = cosine[...], sine[...]
    kv[place.s, pl.ds(0, ROWS)] = turn(acc[:, 512:640], c, s).astype(BF16)
    kv[place.s, pl.ds(ROWS, ROWS)] = acc[:, 640:768].astype(BF16)
    x_kv = remote(kv.at[place.s], kv.at[place.s], x_ss.at[0], x_rs.at[0], place.xdev())
    x_kv.start()
    mine = gather_column(place, kv, place.xh, 0, kv_ss, kv_rs, sends)
    run(mine, 1)
    for h in range(QUERY_PER_KEY):
        q_out[pl.ds(h * ROWS, ROWS)] = turn(
            acc[:, h * HEAD_SIZE : (h + 1) * HEAD_SIZE], c, s
        ).astype(BF16)
    other = (1 - place.xh) * NZ + place.z
    remote(kv.at[other], kv.at[other], x_ss.at[0], x_rs.at[0], place.xdev()).wait_recv()
    sends.append(x_kv)
    theirs = gather_column(place, kv, 1 - place.xh, 1, kv_ss, kv_rs, sends)
    run(theirs, 1)
    x_tok = []
    for i in range(2):
        copy = remote(
            tok_all.at[2 * (1 - place.xh) + i],
            tok_other.at[i],
            x_ss.at[1 + i],
            x_rs.at[1 + i],
            place.xdev(),
        )
        copy.start()
        x_tok.append(copy)
    run(mine, 1)
    run(theirs, 1)
    load_wo.wait()

    def merged_term(source):
        columns = pl.ds(pl.multiple_of(source * WIDTH, WIDTH), WIDTH)
        return dot(up_all[source], wo[:, columns], 1, 1)

    grad = merged_term(t)
    grad = grad + merged_term(arrived(up_all, 1, up_ss, up_rs))
    run(mine, 1)
    run(theirs, 1)
    grad = grad + merged_term(arrived(up_all, 3, up_ss, up_rs))
    run(mine, 1)
    run(theirs, 1)
    grad = grad + merged_term(arrived(up_all, 2, up_ss, up_rs))
    for h in range(QUERY_PER_KEY):
        do_out[pl.ds(h * ROWS, ROWS)] = grad[:, h * HEAD_SIZE : (h + 1) * HEAD_SIZE].astype(BF16)
    run(mine)
    run(theirs)
    for copy in x_tok:
        copy.wait()
    for copy in sends:
        copy.wait_send()


def project(tok, up, wq, wo, cosine, sine):
    vmem = pl.BlockSpec(memory_space=pltpu.VMEM)
    hbm = pl.BlockSpec(memory_space=pl.ANY)
    shape = jax.ShapeDtypeStruct
    dma = pltpu.SemaphoreType.DMA
    return pl.pallas_call(
        project_kernel,
        name="project",
        out_shape=[
            shape((QROWS, HEAD_SIZE), BF16),
            shape((2 * NZ, 2 * ROWS, HEAD_SIZE), BF16),
            shape((QROWS, HEAD_SIZE), BF16),
            shape((NT, ROWS, WIDTH), BF16),
            shape((NT, ROWS, WIDTH), BF16),
            shape((2, ROWS, WIDTH), BF16),
        ],
        in_specs=[vmem, vmem, hbm, hbm, vmem, vmem],
        out_specs=[vmem] * 6,
        scratch_shapes=[
            pltpu.VMEM(wq.shape, BF16),
            pltpu.VMEM(wo.shape, BF16),
            dma((5,)),
            dma((3,)),
            dma((3,)),
            dma((3,)),
            dma((3,)),
            dma((3,)),
            dma((3,)),
            dma((2, 2, 4)),
            dma((2, 2, 4)),
        ],
        compiler_params=pltpu.CompilerParams(
            collective_id=0, has_side_effects=True, vmem_limit_bytes=VMEM_LIMIT
        ),
    )(tok, up, wq, wo, cosine, sine)


def attend_kernel(
    q, kv, do, cosine, sine, expo,
    merged, gq, dkv,
    top, total, acc, logsum, delta, dq,
):
    s = lax.axis_index("seq")
    chunks = [pl.ds(c * CHUNK, CHUNK) for c in range(QROWS // CHUNK)]
    top[...] = jnp.full(top.shape, -1e30, F32)
    total[...] = jnp.zeros(total.shape, F32)
    acc[...] = jnp.zeros(acc.shape, F32)
    dq[...] = jnp.zeros(dq.shape, F32)

    def allowed(c):
        key = lax.broadcasted_iota(jnp.int32, (ROWS, CHUNK), 0)
        query = lax.broadcasted_iota(jnp.int32, (ROWS, CHUNK), 1) + c * CHUNK
        return key <= lax.rem(query, ROWS)

    def forward(j, masked):
        keys = kv[j, pl.ds(0, ROWS)]
        values = kv[j, pl.ds(ROWS, ROWS)]
        for c, cut in enumerate(chunks):
            scores = dot(keys, q[cut], 1, 1)
            if masked:
                scores = jnp.where(allowed(c), scores, -jnp.inf)
            before = top[:, cut]
            now = jnp.maximum(before, jnp.max(scores, axis=0, keepdims=True))
            weights = jnp.exp2((scores - now) * SCALE2)
            alpha = jnp.exp2((before - now) * SCALE2)
            top[:, cut] = now
            total[:, cut] = total[:, cut] * alpha + jnp.sum(weights, axis=0, keepdims=True)
            acc[:, cut] = acc[:, cut] * alpha + dot(values, weights.astype(BF16), 0, 0)

    @pl.loop(0, s)
    def _(j):
        forward(j, False)

    forward(s, True)
    out_t = (acc[...] / total[...]).astype(BF16)
    logsum[...] = top[...] * SCALE2 + jnp.log2(total[...])
    do_t = do[...].astype(F32).T
    delta[...] = jnp.sum(do_t * out_t.astype(F32), axis=0, keepdims=True)
    out = out_t.astype(F32).T.astype(BF16)
    for h in range(QUERY_PER_KEY):
        merged[:, h * HEAD_SIZE : (h + 1) * HEAD_SIZE] = out[h * ROWS : (h + 1) * ROWS]

    def backward(j, masked):
        keys = kv[j, pl.ds(0, ROWS)]
        values = kv[j, pl.ds(ROWS, ROWS)]
        dk = jnp.zeros((ROWS, HEAD_SIZE), F32)
        dv = jnp.zeros((ROWS, HEAD_SIZE), F32)
        for c, cut in enumerate(chunks):
            scores = dot(keys, q[cut], 1, 1)
            probs = jnp.exp2(scores * SCALE2 - logsum[:, cut])
            if masked:
                probs = jnp.where(allowed(c), probs, 0.0)
            grad_probs = dot(values, do[cut], 1, 1)
            grad_scores = (probs * (grad_probs - delta[:, cut])).astype(BF16)
            dv = dv + dot(probs.astype(BF16), do[cut], 1, 0)
            dk = dk + dot(grad_scores, q[cut], 1, 0)
            dq[:, cut] += dot(keys, grad_scores, 0, 0)
        dkv[j, pl.ds(0, ROWS)] = (dk * SCALE).astype(BF16)
        dkv[j, pl.ds(ROWS, ROWS)] = dv.astype(BF16)

    @pl.loop(0, s)
    def _(j):
        backward(j, False)

    backward(s, True)

    @pl.loop(s + 1, 2 * NZ)
    def _(j):
        dkv[j] = jnp.zeros((2 * ROWS, HEAD_SIZE), BF16)

    grad = dq[...].T * SCALE
    c, s_ = cosine[...], sine[...]
    for h in range(QUERY_PER_KEY):
        e = expo[:, h : h + 1]
        sent = jnp.clip(grad[h * ROWS : (h + 1) * ROWS] * jnp.exp2(-e), -127.0, 127.0).astype(BF16)
        gq[:, h * HEAD_SIZE : (h + 1) * HEAD_SIZE] = turn(
            sent.astype(F32) * jnp.exp2(e), c, -s_
        ).astype(BF16)


def attend(q, kv, do, cosine, sine, expo):
    vmem = pl.BlockSpec(memory_space=pltpu.VMEM)
    shape = jax.ShapeDtypeStruct
    return pl.pallas_call(
        attend_kernel,
        name="attend",
        out_shape=[
            shape((ROWS, QUERY_PER_KEY * HEAD_SIZE), BF16),
            shape((ROWS, QUERY_PER_KEY * HEAD_SIZE), BF16),
            shape((2 * NZ, 2 * ROWS, HEAD_SIZE), BF16),
        ],
        in_specs=[vmem] * 6,
        out_specs=[vmem] * 3,
        scratch_shapes=[
            pltpu.VMEM((1, QROWS), F32),
            pltpu.VMEM((1, QROWS), F32),
            pltpu.VMEM((HEAD_SIZE, QROWS), F32),
            pltpu.VMEM((1, QROWS), F32),
            pltpu.VMEM((1, QROWS), F32),
            pltpu.VMEM((HEAD_SIZE, QROWS), F32),
        ],
        compiler_params=pltpu.CompilerParams(vmem_limit_bytes=VMEM_LIMIT),
    )(q, kv, do, cosine, sine, expo)


def finish_kernel(
    merged, gq, dkv, tok_all, up_all, tok_other, wq_hbm, wo_hbm, cosine, sine, expo,
    attended, grad_tokens, gwq, gwo,
    wq, wo, merged_other, up_other, gqkv, kv_own, kv_out, kv_in,
    att_own, att_s, att_r, tok_own, tok_s, tok_r,
    kv_sb, kv_rb, o_sb, o_rb, q_sb, q_rb,
    load_sem, x_ss, x_rs, y_ss, y_rs, kv_ss, kv_rs, o_ss, o_rs, q_ss, q_rs,
):
    place = Place()
    t, xh = place.t, place.xh
    load_wo = pltpu.make_async_copy(wo_hbm, wo, load_sem.at[0])
    load_wo.start()
    load_wq = pltpu.make_async_copy(wq_hbm, wq, load_sem.at[1])
    load_wq.start()
    place.enter()
    sends = []

    def swap(src, dst, i):
        copy = remote(src, dst, x_ss.at[i], x_rs.at[i], place.xdev())
        copy.start()
        return copy

    x_merged = swap(merged, merged_other, 0)
    x_up = [swap(up_all.at[2 * (1 - xh) + i], up_other.at[i], 1 + i) for i in range(2)]

    def load_kv(dest, sub, part):
        ref = dkv.at[((1 - xh) if sub == 0 else xh) * NZ + dest]
        if part is not None:
            return ref[pl.ds(part * ROWS, ROWS)].astype(F32)
        return ref[...].astype(F32)

    def done_kv(sub, value):
        if sub == 0:
            kv_out[...] = value.astype(BF16)
        else:
            kv_own[...] = value

    ring_kv = scatter_ring(
        place, 2, 2 * ROWS, load_kv, kv_sb, kv_rb, kv_ss, kv_rs, sends, done_kv
    )
    run(ring_kv, 2)

    def scatter_tensor(term, own, sbuf, rbuf, which):
        for offset in (1, 3, 2):
            sbuf[offset - 1] = term(lax.rem(t + offset, NT)).astype(BF16)
            copy = remote(
                sbuf.at[offset - 1],
                rbuf.at[offset - 1],
                y_ss.at[which, offset - 1],
                y_rs.at[which, offset - 1],
                place.tensor(offset),
            )
            copy.start()
            sends.append(copy)
        own[...] = term(t)

    def collect_tensor(own, rbuf, which, out):
        value = own[...]
        for offset in (1, 3, 2):
            ref = rbuf.at[offset - 1]
            remote(
                ref,
                ref,
                y_ss.at[which, offset - 1],
                y_rs.at[which, offset - 1],
                place.tensor(offset),
            ).wait_recv()
            value = value + ref[...]
        out[...] = value.astype(BF16)

    def attended_term(dest):
        return dot(merged[...], wo[:, pl.ds(pl.multiple_of(dest * WIDTH, WIDTH), WIDTH)], 1, 0)

    def tokens_term(dest):
        return dot(gqkv[0], wq[pl.ds(pl.multiple_of(dest * WIDTH, WIDTH), WIDTH)], 1, 1)

    load_wo.wait()
    scatter_tensor(attended_term, att_own, att_s, att_r, 0)
    run(ring_kv)
    x_kv = swap(kv_out, kv_in, 3)
    c, s = cosine[...], sine[...]
    gqkv[0, :, 0:512] = gq[...]
    x_kv.wait()
    grad = kv_own[...] + kv_in[...]

    def squeeze(value, column):
        e = expo[:, column : column + 1]
        sent = jnp.clip(value * jnp.exp2(-e), -127.0, 127.0).astype(BF16)
        return sent.astype(F32) * jnp.exp2(e)

    gqkv[0, :, 512:640] = turn(squeeze(grad[:ROWS], 4), c, -s).astype(BF16)
    gqkv[0, :, 640:768] = squeeze(grad[ROWS:], 5).astype(BF16)
    x_gqkv = swap(gqkv.at[0], gqkv.at[1], 4)
    load_wq.wait()
    scatter_tensor(tokens_term, tok_own, tok_s, tok_r, 1)

    def columns(dest):
        return pl.ds(pl.multiple_of(lax.rem(dest, 4) * 256, 256), 256)

    def load_o(dest, sub, part):
        first = sub * 256 + (0 if part is None else part * 128)
        last = first + (256 if part is None else 128)
        shard = lax.div(dest, 4)
        value = dot(merged[:, first:last], up_all[2 * xh + shard, :, columns(dest)], 0, 0)
        return value + dot(
            merged_other[:, first:last], up_other[shard, :, columns(dest)], 0, 0
        )

    def done_o(sub, value):
        gwo[pl.ds(sub * 256, 256)] = value.astype(BF16)

    def load_q(dest, sub, part):
        shard = lax.div(dest, 4)
        left = tok_all[2 * xh + shard, :, columns(dest)]
        left_other = tok_other[shard, :, columns(dest)]
        if part is not None:
            left = left[:, part * 128 : (part + 1) * 128]
            left_other = left_other[:, part * 128 : (part + 1) * 128]
        cut = slice(sub * 256, (sub + 1) * 256)
        return dot(left, gqkv[0, :, cut], 0, 0) + dot(left_other, gqkv[1, :, cut], 0, 0)

    def done_q(sub, value):
        gwq[:, sub * 256 : (sub + 1) * 256] = value.astype(BF16)

    x_merged.wait()
    for copy in x_up:
        copy.wait()
    ring_o = scatter_ring(place, 2, 256, load_o, o_sb, o_rb, o_ss, o_rs, sends, done_o)
    ring_q = scatter_ring(place, 3, 256, load_q, q_sb, q_rb, q_ss, q_rs, sends, done_q)
    run(ring_o, 6)
    x_gqkv.wait()
    run(ring_q, 3)
    run(ring_o)
    collect_tensor(att_own, att_r, 0, attended)
    run(ring_q, 6)
    collect_tensor(tok_own, tok_r, 1, grad_tokens)
    run(ring_q)
    for copy in sends:
        copy.wait_send()


def finish(merged, gq, dkv, tok_all, up_all, tok_other, wq, wo, cosine, sine, expo):
    vmem = pl.BlockSpec(memory_space=pltpu.VMEM)
    hbm = pl.BlockSpec(memory_space=pl.ANY)
    shape = jax.ShapeDtypeStruct
    dma = pltpu.SemaphoreType.DMA
    ring = pltpu.VMEM
    return pl.pallas_call(
        finish_kernel,
        name="finish",
        out_shape=[
            shape((ROWS, WIDTH), BF16),
            shape((ROWS, WIDTH), BF16),
            shape((256, 768), BF16),
            shape((512, 256), BF16),
        ],
        in_specs=[vmem] * 6 + [hbm] * 2 + [vmem] * 3,
        out_specs=[vmem] * 4,
        scratch_shapes=[
            pltpu.VMEM(wq.shape, BF16),
            pltpu.VMEM(wo.shape, BF16),
            pltpu.VMEM((ROWS, 512), BF16),
            pltpu.VMEM((2, ROWS, WIDTH), BF16),
            pltpu.VMEM((2, ROWS, 768), BF16),
            pltpu.VMEM((2 * ROWS, HEAD_SIZE), F32),
            pltpu.VMEM((2 * ROWS, HEAD_SIZE), BF16),
            pltpu.VMEM((2 * ROWS, HEAD_SIZE), BF16),
            pltpu.VMEM((ROWS, WIDTH), F32),
            pltpu.VMEM((3, ROWS, WIDTH), BF16),
            pltpu.VMEM((3, ROWS, WIDTH), BF16),
            pltpu.VMEM((ROWS, WIDTH), F32),
            pltpu.VMEM((3, ROWS, WIDTH), BF16),
            pltpu.VMEM((3, ROWS, WIDTH), BF16),
            ring((2, 4, 2, 2 * ROWS, HEAD_SIZE), BF16),
            ring((2, 4, 2, 2 * ROWS, HEAD_SIZE), BF16),
            ring((2, 4, 2, 256, 256), BF16),
            ring((2, 4, 2, 256, 256), BF16),
            ring((2, 4, 3, 256, 256), BF16),
            ring((2, 4, 3, 256, 256), BF16),
            dma((2,)),
            dma((5,)),
            dma((5,)),
            dma((2, 3)),
            dma((2, 3)),
            dma((2, 4, 2)),
            dma((2, 4, 2)),
            dma((2, 4, 2)),
            dma((2, 4, 2)),
            dma((2, 4, 3)),
            dma((2, 4, 3)),
        ],
        compiler_params=pltpu.CompilerParams(
            collective_id=1, has_side_effects=True, vmem_limit_bytes=VMEM_LIMIT
        ),
    )(merged, gq, dkv, tok_all, up_all, tok_other, wq, wo, cosine, sine, expo)


def local(tokens, input_projection_weight, w_out, upstream, exponents):
    seq_index = lax.axis_index("seq")
    half = HEAD_SIZE // 2
    freqs = jnp.power(F32(THETA), -jnp.arange(half, dtype=F32) * 2.0 / HEAD_SIZE)
    places = seq_index * ROWS + jnp.arange(ROWS, dtype=jnp.int32)
    angles = places.astype(F32)[:, None] * freqs[None, :]
    cosine = jnp.tile(jnp.cos(angles), (1, 2))
    sine = jnp.sin(angles)
    sine = jnp.concatenate([-sine, sine], axis=1)
    groups = ROWS // SCALE_TOKENS
    mine = lax.dynamic_slice_in_dim(exponents, seq_index * groups, groups, 0).astype(F32)
    expo = jnp.repeat(mine, SCALE_TOKENS, axis=0)
    q, kv, do, tok_all, up_all, tok_other = project(
        tokens, upstream, input_projection_weight, w_out, cosine, sine
    )
    merged, gq, dkv = attend(q, kv, do, cosine, sine, expo)
    return finish(
        merged,
        gq,
        dkv,
        tok_all,
        up_all,
        tok_other,
        input_projection_weight,
        w_out,
        cosine,
        sine,
        expo,
    )


def solution(mesh):
    in_specs = (
        P(("dp", "seq"), "tensor"),
        P(None, "tensor"),
        P("tensor", None),
        P(("dp", "seq"), "tensor"),
        P("dp", "tensor"),
    )
    out_specs = (
        P(("dp", "seq"), "tensor"),
        P(("dp", "seq"), "tensor"),
        P(("dp", "seq"), "tensor"),
        P(("dp", "tensor"), "seq"),
    )
    return jax.shard_map(local, mesh=mesh, in_specs=in_specs, out_specs=out_specs, check_vma=False)
```

time: 1140 us -> 175 us (0.15)
  waiting for transfers between devices: 884 us -> 0 us
  Pallas kernels: 0 us -> 166 us
  blocking collectives: 109 us -> 0 us
  matrix products: 65.7 us -> 0 us
  starting transfers between devices: 22.5 us -> 0 us
  other arithmetic: 20.2 us -> 1.95 us
  local copies, waits for them, and re-layouts: 21.9 us -> 6.62 us
  between operations: 14.7 us -> 0.71 us
    reduce_scatter x6 -> x0, waiting for transfers between devices: 840 us -> none  [the longest x1 216 us: local(): lax.psum_scatter(weight_acc.astype(jnp.bfloat16), 'seq', scatter_dimensio...]
    pallas_call x0 -> x3, Pallas kernels: none -> 166 us  [the longest x1 103 us: finish(): pl.pallas_call(finish_kernel, name='finish', out_shape=[shape((ROWS, WIDT...]
    all_gather x2 -> x0, blocking collectives: 90.9 us -> none  [the longest x1 47.7 us: local(): lax.all_gather(keys, 'seq', axis=0, tiled=True)]
    dot_general x27 -> x0, matrix products: 65.7 us -> none  [the longest x9 27.4 us: dot_cols(): lax.dot_general(left, right, (((0,), (0,)), ((), ())), preferred_element_...]
    all_gather x2 -> x0, waiting for transfers between devices: 31.8 us -> none  [the longest x1 31.8 us: local(): lax.all_gather(tokens, 'tensor', axis=1, tiled=True)]
    all_to_all x3 -> x0, starting transfers between devices: 22 us -> none  [the longest x1 9.62 us: local(): lax.all_to_all(wire_heads, 'seq', split_axis=1, concat_axis=0, tiled=True)]
    all_to_all x1 -> x0, blocking collectives: 17.9 us -> none  [local(): lax.all_to_all(out_heads, 'seq', split_axis=1, concat_axis=0, tiled=True)]
  transfers between devices with their start and end apart: 11 -> 0, of which waited for: 8 -> 0; matrix products, arithmetic and copies ran while one was open for 5% -> 0% of each run, Pallas kernels for 0% -> 0%
where the time goes in v1:
time: 175 us
  Pallas kernels  166 us (95%)
  local copies, waits for them, and re-layouts  6.62 us (4%)
  other arithmetic  1.95 us (1%)
    pallas_call x1, Pallas kernels, finish(): pl.pallas_call(finish_kernel, name='finish', out_shape=[shape((ROWS, WIDT...  103 us
    pallas_call x1, Pallas kernels, project(): pl.pallas_call(project_kernel, name='project', out_shape=[shape((QROWS, H...  57 us
    pallas_call x1, Pallas kernels, attend(): pl.pallas_call(attend_kernel, name='attend', out_shape=[shape((ROWS, QUER...  5.54 us
    unnamed x8, local copies, waits for them, and re-layouts  5.05 us

profile of v1, /device:TPU:2, one launch (start us, length us, event | category | flops | bytes accessed | tf_op | source)
XLA Modules:
  0.0 174.9 jit_solution(5345470779587414665)
XLA Ops:
  0.7 0.8 dynamic-slice_convert_fusion
  1.4 0.1 copy.18
  1.5 0.6 broadcast_in_dim.2
  2.2 0.4 fusion
  2.6 0.7 pad_maximum_fusion.sine
  3.3 0.1 copy.16
  3.4 0.7 copy.17.cosine
  4.2 57.0 %project.1 = (bf16[768,128]{1,0:T(8,128)(2,1)}, bf16[16,384,128]{2,1,0:T(8,128)(2,1)}, bf16[768,128]{1,0:T(8,128)(2,1)}, bf16[4,192,1024]{2,1,0:T(8,128)(2,1)}, ...) custom-call(bf16[192,1024]{1,0:T(8,128)(2,1)} %tok.1, bf16[192,1024]{1,0:T(8,128)(2,1)} %up.1, ...), custom_call_target="tpu_custom_call" | custom-call | tf_op jit(solution)/shard_map/project/pallas_call | solution.py:266
  61.2 5.5 %attend.1 = (bf16[192,512]{1,0:T(8,128)(2,1)}, bf16[192,512]{1,0:T(8,128)(2,1)}, bf16[16,384,128]{2,1,0:T(8,128)(2,1)}) custom-call(bf16[768,128]{1,0:T(8,128)(2,1)} %get-tuple-element.13.q, bf16[16,384,128]{2,1,0:T(8,128)(2,1)} %get-tuple-element.14.kv, bf16[768,128]{1,0:T(8,128)(2,1)} %get-tuple-element.15.do, f32[192,128]{1,0:T(8,128)} %copy.17.cosine, ...), custom_call_target="tpu_custom_call" | custom-call | tf_op jit(solution)/shard_map/attend/pallas_call | solution.py:384
  66.7 103.1 %finish.1 = (bf16[192,1024]{1,0:T(8,128)(2,1)}, bf16[192,1024]{1,0:T(8,128)(2,1)}, bf16[256,768]{1,0:T(8,128)(2,1)}, bf16[512,256]{1,0:T(8,128)(2,1)}) custom-call(bf16[192,512]{1,0:T(8,128)(2,1)} %get-tuple-element.16.merged, bf16[192,512]{1,0:T(8,128)(2,1)} %get-tuple-element.17.gq, bf16[16,384,128]{2,1,0:T(8,128)(2,1)} %get-tuple-element.18.dkv, ...), custom_call_target="tpu_custom_call" | custom-call | tf_op jit(solution)/shard_map/finish/pallas_call | solution.py:553
  169.8 0.0 copy-start
  169.8 0.0 copy-start.1
  169.8 1.8 %copy.25 = bf16[192,1024]{1,0:T(8,128)(2,1)} copy(bf16[192,1024]{1,0:T(8,128)(2,1)} %get-tuple-element.29) | data formatting | bytes 786432
  171.6 1.8 %copy.26 = bf16[192,1024]{1,0:T(8,128)(2,1)} copy(bf16[192,1024]{1,0:T(8,128)(2,1)} %get-tuple-element.30) | data formatting | bytes 786432
  173.4 0.0 copy-done
  173.4 0.7 copy.27
  174.1 0.0 copy-done.1
  174.1 0.7 copy.28
  (3 shorter events, 0.0 us)
Async XLA Ops:
  169.8 3.6 %copy-start = (bf16[256,768]{1,0:T(8,128)(2,1)S(1)}, bf16[256,768]{1,0:T(8,128)(2,1)}, u32[]{:S(2)}) copy-start(bf16[256,768]{1,0:T(8,128)(2,1)} %get-tuple-element.31) | copy-start | bytes 1179652
  169.8 4.4 %copy-start.1 = (bf16[512,256]{1,0:T(8,128)(2,1)S(1)}, bf16[512,256]{1,0:T(8,128)(2,1)}, u32[]{:S(2)}) copy-start(bf16[512,256]{1,0:T(8,128)(2,1)} %get-tuple-element.32) | copy-start | bytes 786436

commit v2 on v1

v2 whole, which is shorter than its diff:
```python
import functools
import math

import jax
import jax.numpy as jnp
from jax import lax
from jax.experimental import pallas as pl
from jax.experimental.pallas import tpu as pltpu
from jax.sharding import PartitionSpec as P

HEAD_SIZE = 128
QUERY_PER_KEY = 4
SCALE_TOKENS = 16
THETA = 500000.0

NZ = 8
NT = 4
ROWS = 192
QROWS = QUERY_PER_KEY * ROWS
PAIR = 2 * ROWS
WIDTH = 1024
MESH = pl.DeviceIdType.MESH
BF16 = jnp.bfloat16
F32 = jnp.float32
SCALE = 1.0 / math.sqrt(HEAD_SIZE)
SCALE2 = SCALE * math.log2(math.e)
VMEM_LIMIT = 60 * 2**20


def dot(left, right, left_dim, right_dim):
    return lax.dot_general(
        left, right, (((left_dim,), (right_dim,)), ((), ())), preferred_element_type=F32
    )


class Place:
    def __init__(self):
        self.d = lax.axis_index("dp")
        self.s = lax.axis_index("seq")
        self.t = lax.axis_index("tensor")
        self.xh = lax.div(self.s, NZ)
        self.z = lax.rem(self.s, NZ)

    def tensor(self, offset):
        return (self.d, self.s, lax.rem(self.t + offset, NT))

    def zdev(self, sign):
        return (self.d, self.xh * NZ + lax.rem(self.z + sign + NZ, NZ), self.t)

    def xdev(self):
        return (self.d, (1 - self.xh) * NZ + self.z, self.t)

    def enter(self):
        barrier = pltpu.get_barrier_semaphore()
        partners = [self.tensor(1), self.tensor(2), self.tensor(3)]
        partners += [self.zdev(1), self.zdev(-1), self.xdev()]
        for partner in partners:
            pl.semaphore_signal(barrier, inc=1, device_id=partner, device_id_type=MESH)
        pl.semaphore_wait(barrier, len(partners))


def remote(src, dst, send_sem, recv_sem, device):
    return pltpu.make_async_remote_copy(
        src_ref=src,
        dst_ref=dst,
        send_sem=send_sem,
        recv_sem=recv_sem,
        device_id=device,
        device_id_type=MESH,
    )


def turn(vectors, cosine, sine):
    return vectors * cosine + pltpu.roll(vectors, HEAD_SIZE // 2, 1) * sine


def gather_column(place, kv, column, which, ss, rs, sends):
    cut = pl.ds(pl.multiple_of(column * ROWS, ROWS), ROWS)

    def part(step, di, z):
        z = lax.rem(z + 2 * NZ, NZ)
        return kv.at[di, z, cut] if step == 4 else kv.at[:, z, cut]

    def arrived(step, di, sign):
        ref = part(step, di, place.z - sign * step)
        sem = rs.at[which, di, step - 1]
        remote(ref, ref, ss.at[which, di, step - 1], sem, place.zdev(sign)).wait_recv()

    for step in range(1, 5):
        for di, sign in ((0, 1), (1, -1)):
            if step > 1:
                arrived(step - 1, di, sign)
            ref = part(step, di, place.z - sign * (step - 1))
            copy = remote(
                ref,
                ref,
                ss.at[which, di, step - 1],
                rs.at[which, di, step - 1],
                place.zdev(sign),
            )
            copy.start()
            sends.append(copy)
        yield
    for di, sign in ((0, 1), (1, -1)):
        arrived(4, di, sign)


def scatter_ring(place, subs, rows, load, sbuf, rbuf, ss, rs, sends, done):
    half = rows // 2
    for step in (4, 3, 2, 1):
        for sub in subs:
            for di, sign in ((0, 1), (1, -1)):
                dest = lax.rem(place.z + sign * step + NZ, NZ)
                cut = pl.ds(di * half, half)
                here = sbuf.at[di, step - 1, sub]
                there = rbuf.at[di, step - 1, sub]
                if step == 4:
                    here, there = here.at[cut], there.at[cut]
                    here[...] = load(dest, sub, di).astype(BF16)
                else:
                    value = load(dest, sub, None)
                    before = rbuf.at[di, step, sub]
                    if step == 3:
                        before = before.at[cut]
                    remote(
                        before, before, ss.at[di, step, sub], rs.at[di, step, sub], place.zdev(sign)
                    ).wait_recv()
                    if step == 3:
                        here[cut] = (value[di * half : (di + 1) * half] + before[...]).astype(BF16)
                        rest = 1 - di
                        here[pl.ds(rest * half, half)] = value[
                            rest * half : (rest + 1) * half
                        ].astype(BF16)
                    else:
                        here[...] = (value + before[...]).astype(BF16)
                copy = remote(
                    here, there, ss.at[di, step - 1, sub], rs.at[di, step - 1, sub], place.zdev(sign)
                )
                copy.start()
                sends.append(copy)
            yield
    for sub in subs:
        total = load(place.z, sub, None)
        for di, sign in ((0, 1), (1, -1)):
            ref = rbuf.at[di, 0, sub]
            remote(ref, ref, ss.at[di, 0, sub], rs.at[di, 0, sub], place.zdev(sign)).wait_recv()
            total = total + ref[...]
        done(sub, total)


def run(steps, count=None):
    if count is None:
        for _ in steps:
            pass
    else:
        for _ in range(count):
            next(steps)


def layer_kernel(
    tok, up, wq_hbm, wo_hbm, freqs, exponents,
    attended, grad_tokens, gwq, gwo,
    wq, wo, tok_all, up_all, tok_other, up_other, cosine, sine, expo,
    q, kv, do, merged, merged_other, gqkv,
    key_place, limit, top, total, acc, logsum, delta, dq,
    dkv, kv_own, kv_out, kv_in,
    att_own, att_s, att_r, tok_own, tok_s, tok_r,
    kv_sb, kv_rb, o_sb, o_rb, q_sb, q_rb,
    load_sem, y_ss, y_rs, x_ss, x_rs, ag_ss, ag_rs,
    kv_ss, kv_rs, o_ss, o_rs, q_ss, q_rs,
):
    place = Place()
    t, xh, z = place.t, place.xh, place.z
    loads = []
    for i in range(NT):
        rows = pl.ds(pl.multiple_of(lax.rem(t + (0, 1, 3, 2)[i], NT) * WIDTH, WIDTH), WIDTH)
        loads.append(pltpu.make_async_copy(wq_hbm.at[rows], wq.at[rows], load_sem.at[i]))
        loads[-1].start()
    load_wo = pltpu.make_async_copy(wo_hbm, wo, load_sem.at[4])
    load_wo.start()
    place.enter()
    sends = []

    def swap(src, dst, i):
        copy = remote(src, dst, x_ss.at[i], x_rs.at[i], place.xdev())
        copy.start()
        return copy

    def spread(own, everyone, which):
        copies = []
        for offset in (1, 3, 2):
            copy = remote(
                own,
                everyone.at[t],
                y_ss.at[which, offset - 1],
                y_rs.at[which, offset - 1],
                place.tensor(offset),
            )
            copy.start()
            copies.append(copy)
        return copies

    def arrived(everyone, offset, which):
        source = lax.rem(t + NT - offset, NT)
        ref = everyone.at[source]
        remote(
            ref, ref, y_ss.at[which, offset - 1], y_rs.at[which, offset - 1], place.tensor(offset)
        ).wait_recv()
        return source

    def scatter_tensor(term, own, sbuf, rbuf, which):
        for offset in (1, 3, 2):
            sbuf[offset - 1] = term(lax.rem(t + offset, NT)).astype(BF16)
            copy = remote(
                sbuf.at[offset - 1],
                rbuf.at[offset - 1],
                y_ss.at[which, offset - 1],
                y_rs.at[which, offset - 1],
                place.tensor(offset),
            )
            copy.start()
            sends.append(copy)
        own[...] = term(t)

    def collect_tensor(own, rbuf, which, out):
        value = own[...]
        for offset in (1, 3, 2):
            ref = rbuf.at[offset - 1]
            remote(
                ref,
                ref,
                y_ss.at[which, offset - 1],
                y_rs.at[which, offset - 1],
                place.tensor(offset),
            ).wait_recv()
            value = value + ref[...]
        out[...] = value.astype(BF16)

    token_sends = spread(tok, tok_all, 0)
    tok_all[t] = tok[...]
    up_all[t] = up[...]
    position = lax.broadcasted_iota(jnp.int32, (ROWS, HEAD_SIZE), 0) + place.s * ROWS
    angles = position.astype(F32) * freqs[...]
    cosine[...] = jnp.cos(angles)
    low = lax.broadcasted_iota(jnp.int32, (ROWS, HEAD_SIZE), 1) < HEAD_SIZE // 2
    sines = jnp.sin(angles)
    sine[...] = jnp.where(low, -sines, sines)
    groups = exponents.shape[0]
    group = lax.broadcasted_iota(jnp.int32, (ROWS, groups), 0) // SCALE_TOKENS
    group = group + place.s * (ROWS // SCALE_TOKENS)
    pick = lax.broadcasted_iota(jnp.int32, (ROWS, groups), 1) == group
    expo[...] = dot(pick.astype(F32).astype(BF16), exponents[...].astype(F32).astype(BF16), 1, 0)
    row = lax.broadcasted_iota(jnp.int32, (PAIR, HEAD_SIZE), 0)
    key_place[...] = jnp.where(row < ROWS, row, row + (NZ - 1) * ROWS)
    limit[...] = place.s * ROWS + lax.rem(
        lax.broadcasted_iota(jnp.int32, (1, QROWS), 1), jnp.int32(ROWS)
    )
    top[...] = jnp.full(top.shape, -jnp.inf, F32)
    total[...] = jnp.zeros(total.shape, F32)
    acc[...] = jnp.zeros(acc.shape, F32)
    dq[...] = jnp.zeros(dq.shape, F32)
    loads[0].wait()
    projected = dot(tok[...], wq[pl.ds(pl.multiple_of(t * WIDTH, WIDTH), WIDTH)], 1, 0)
    for load in loads[1:]:
        load.wait()
    for offset in (1, 3, 2):
        source = arrived(tok_all, offset, 0)
        rows = pl.ds(pl.multiple_of(source * WIDTH, WIDTH), WIDTH)
        if offset == 2:
            for copy in token_sends:
                copy.wait_send()
            sends.extend(spread(up, up_all, 1))
        projected = projected + dot(tok_all[source], wq[rows], 1, 0)

    c, s = cosine[...], sine[...]
    mine = pl.ds(pl.multiple_of(xh * ROWS, ROWS), ROWS)
    kv[0, z, mine] = turn(projected[:, 512:640], c, s).astype(BF16)
    kv[1, z, mine] = projected[:, 640:768].astype(BF16)
    x_kv = swap(kv.at[:, z, mine], kv.at[:, z, mine], 0)
    own_ring = gather_column(place, kv, xh, 0, ag_ss, ag_rs, sends)
    run(own_ring, 1)
    for h in range(QUERY_PER_KEY):
        q[pl.ds(h * ROWS, ROWS)] = turn(
            projected[:, h * HEAD_SIZE : (h + 1) * HEAD_SIZE], c, s
        ).astype(BF16)
    theirs = pl.ds(pl.multiple_of((1 - xh) * ROWS, ROWS), ROWS)
    other = kv.at[:, z, theirs]
    remote(other, other, x_ss.at[0], x_rs.at[0], place.xdev()).wait_recv()
    sends.append(x_kv)
    other_ring = gather_column(place, kv, 1 - xh, 1, ag_ss, ag_rs, sends)
    run(other_ring, 1)
    x_tok = [swap(tok_all.at[2 * (1 - xh)], tok_other.at[0], 1)]

    def around(step):
        return lax.rem(z + step + NZ, NZ)

    def forward(zk):
        keys = kv[0, zk]
        values = kv[1, zk]
        for cut in range(0, QROWS, HEAD_SIZE):
            cut = slice(cut, cut + HEAD_SIZE)
            scores = dot(keys, q[cut], 1, 1)
            allowed = key_place[...] <= limit[:, cut] - zk * ROWS
            scores = jnp.where(allowed, scores, -jnp.inf)
            before = top[:, cut]
            now = jnp.maximum(before, jnp.max(scores, axis=0, keepdims=True))
            weights = jnp.exp2((scores - now) * SCALE2)
            alpha = jnp.exp2((before - now) * SCALE2)
            top[:, cut] = now
            total[:, cut] = total[:, cut] * alpha + jnp.sum(weights, axis=0, keepdims=True)
            acc[:, cut] = acc[:, cut] * alpha + dot(values, weights.astype(BF16), 0, 0)

    def merged_term(source):
        columns = pl.ds(pl.multiple_of(source * WIDTH, WIDTH), WIDTH)
        return dot(up_all[source], wo[:, columns], 1, 1)

    def step_rings():
        run(own_ring, 1)
        run(other_ring, 1)

    forward(z)
    step_rings()
    forward(around(1))
    forward(around(-1))
    load_wo.wait()
    step_rings()
    forward(around(2))
    forward(around(-2))
    grad = merged_term(t)
    grad = grad + merged_term(arrived(up_all, 1, 1))
    step_rings()
    forward(around(3))
    forward(around(-3))
    grad = grad + merged_term(arrived(up_all, 3, 1))
    grad = grad + merged_term(arrived(up_all, 2, 1))
    x_up = [swap(up_all.at[2 * (1 - xh) + i], up_other.at[i], 2 + i) for i in range(2)]
    for h in range(QUERY_PER_KEY):
        do[pl.ds(h * ROWS, ROWS)] = grad[:, h * HEAD_SIZE : (h + 1) * HEAD_SIZE].astype(BF16)
    run(own_ring)
    run(other_ring)
    forward(around(4))

    out_t = (acc[...] / total[...]).astype(BF16)
    out = out_t.astype(F32).T.astype(BF16)
    for h in range(QUERY_PER_KEY):
        merged[:, h * HEAD_SIZE : (h + 1) * HEAD_SIZE] = out[h * ROWS : (h + 1) * ROWS]
    x_merged = swap(merged, merged_other, 4)
    logsum[...] = top[...] * SCALE2 + jnp.log2(total[...])
    delta[...] = jnp.sum(do[...].astype(F32).T * out_t.astype(F32), axis=0, keepdims=True)

    def backward(zk):
        keys = kv[0, zk]
        values = kv[1, zk]
        dk = jnp.zeros((PAIR, HEAD_SIZE), F32)
        dv = jnp.zeros((PAIR, HEAD_SIZE), F32)
        scores = dot(keys, q[...], 1, 1)
        allowed = key_place[:, 0:1] <= limit[...] - zk * ROWS
        probs = jnp.exp2(jnp.where(allowed, scores * SCALE2 - logsum[...], -jnp.inf))
        grad_probs = dot(values, do[...], 1, 1)
        grad_scores = (probs * (grad_probs - delta[...])).astype(BF16)
        dv = dot(probs.astype(BF16), do[...], 1, 0).astype(BF16)
        dk = (dot(grad_scores, q[...], 1, 0) * SCALE).astype(BF16)
        dq[...] += dot(keys, grad_scores, 0, 0)
        for column in range(2):
            rows = slice(column * ROWS, (column + 1) * ROWS)
            dkv[zk, column, 0:ROWS] = dk[rows]
            dkv[zk, column, ROWS:PAIR] = dv[rows]

    def load_kv(dest, sub, part):
        ref = dkv.at[dest, (1 - xh) if sub == 0 else xh]
        if part is not None:
            return ref[pl.ds(part * ROWS, ROWS)].astype(F32)
        return ref[...].astype(F32)

    def done_kv(sub, value):
        if sub == 0:
            kv_out[...] = value.astype(BF16)
        else:
            kv_own[...] = value

    ring_kv = scatter_ring(
        place, (0, 1), PAIR, load_kv, kv_sb, kv_rb, kv_ss, kv_rs, sends, done_kv
    )

    def attended_term(dest):
        return dot(merged[...], wo[:, pl.ds(pl.multiple_of(dest * WIDTH, WIDTH), WIDTH)], 1, 0)

    backward(around(4))
    run(ring_kv, 2)
    scatter_tensor(attended_term, att_own, att_s, att_r, 2)
    backward(around(3))
    backward(around(-3))
    run(ring_kv, 2)
    backward(around(2))
    backward(around(-2))
    run(ring_kv, 2)
    backward(around(1))
    backward(around(-1))
    run(ring_kv, 2)
    backward(z)

    def squeeze(value, column):
        e = expo[:, column : column + 1]
        sent = jnp.clip(value * jnp.exp2(-e), -127.0, 127.0).astype(BF16)
        return sent.astype(F32) * jnp.exp2(e)

    grad = dq[...].T * SCALE
    for h in range(QUERY_PER_KEY):
        gqkv[0, :, h * HEAD_SIZE : (h + 1) * HEAD_SIZE] = turn(
            squeeze(grad[h * ROWS : (h + 1) * ROWS], h), c, -s
        ).astype(BF16)
    x_gq = swap(gqkv.at[0, :, pl.ds(0, 512)], gqkv.at[1, :, pl.ds(0, 512)], 5)
    x_tok.append(swap(tok_all.at[2 * (1 - xh) + 1], tok_other.at[1], 6))
    run(ring_kv)
    x_dkv = swap(kv_out, kv_in, 7)

    def columns(dest):
        return pl.ds(pl.multiple_of(lax.rem(dest, 4) * 256, 256), 256)

    def load_o(dest, sub, part):
        first = sub * 256 + (0 if part is None else part * 128)
        last = first + (256 if part is None else 128)
        shard = lax.div(dest, 4)
        value = dot(merged[:, first:last], up_all[2 * xh + shard, :, columns(dest)], 0, 0)
        return value + dot(
            merged_other[:, first:last], up_other[shard, :, columns(dest)], 0, 0
        )

    def done_o(sub, value):
        gwo[pl.ds(sub * 256, 256)] = value.astype(BF16)

    def load_q(dest, sub, part):
        shard = lax.div(dest, 4)
        left = tok_all[2 * xh + shard, :, columns(dest)]
        left_other = tok_other[shard, :, columns(dest)]
        if part is not None:
            left = left[:, part * 128 : (part + 1) * 128]
            left_other = left_other[:, part * 128 : (part + 1) * 128]
        cut = slice(sub * 256, (sub + 1) * 256)
        return dot(left, gqkv[0, :, cut], 0, 0) + dot(left_other, gqkv[1, :, cut], 0, 0)

    def done_q(sub, value):
        gwq[:, sub * 256 : (sub + 1) * 256] = value.astype(BF16)

    ring_o = scatter_ring(place, (0, 1), 256, load_o, o_sb, o_rb, o_ss, o_rs, sends, done_o)
    ring_q = scatter_ring(place, (0, 1), 256, load_q, q_sb, q_rb, q_ss, q_rs, sends, done_q)
    ring_k = scatter_ring(place, (2,), 256, load_q, q_sb, q_rb, q_ss, q_rs, sends, done_q)
    for copy in x_up:
        copy.wait()
    x_merged.wait()
    run(ring_o, 4)
    x_dkv.wait()
    grad = kv_own[...] + kv_in[...]
    gqkv[0, :, 512:640] = turn(squeeze(grad[:ROWS], 4), c, -s).astype(BF16)
    gqkv[0, :, 640:768] = squeeze(grad[ROWS:], 5).astype(BF16)
    x_gkv = swap(gqkv.at[0, :, pl.ds(512, 256)], gqkv.at[1, :, pl.ds(512, 256)], 8)
    run(ring_o, 2)

    def tokens_term(dest):
        return dot(gqkv[0], wq[pl.ds(pl.multiple_of(dest * WIDTH, WIDTH), WIDTH)], 1, 1)

    scatter_tensor(tokens_term, tok_own, tok_s, tok_r, 3)
    run(ring_o, 2)
    x_gq.wait()
    for copy in x_tok:
        copy.wait()
    run(ring_q, 2)
    run(ring_o)
    collect_tensor(att_own, att_r, 2, attended)
    run(ring_q, 2)
    x_gkv.wait()
    run(ring_k, 1)
    run(ring_q, 2)
    run(ring_k, 1)
    collect_tensor(tok_own, tok_r, 3, grad_tokens)
    run(ring_q, 2)
    run(ring_k, 2)
    run(ring_q)
    run(ring_k)
    for copy in sends:
        copy.wait_send()


def layer(tok, up, wq, wo, freqs, exponents):
    vmem = pl.BlockSpec(memory_space=pltpu.VMEM)
    hbm = pl.BlockSpec(memory_space=pl.ANY)
    shape = jax.ShapeDtypeStruct
    dma = pltpu.SemaphoreType.DMA
    buf = pltpu.VMEM
    heads = QUERY_PER_KEY * HEAD_SIZE
    return pl.pallas_call(
        layer_kernel,
        name="layer",
        out_shape=[
            shape((ROWS, WIDTH), BF16),
            shape((ROWS, WIDTH), BF16),
            shape((256, 768), BF16),
            shape((512, 256), BF16),
        ],
        in_specs=[vmem, vmem, hbm, hbm, vmem, vmem],
        out_specs=[vmem] * 4,
        scratch_shapes=[
            buf(wq.shape, BF16),
            buf(wo.shape, BF16),
            buf((NT, ROWS, WIDTH), BF16),
            buf((NT, ROWS, WIDTH), BF16),
            buf((2, ROWS, WIDTH), BF16),
            buf((2, ROWS, WIDTH), BF16),
            buf((ROWS, HEAD_SIZE), F32),
            buf((ROWS, HEAD_SIZE), F32),
            buf((ROWS, 6), F32),
            buf((QROWS, HEAD_SIZE), BF16),
            buf((2, NZ, PAIR, HEAD_SIZE), BF16),
            buf((QROWS, HEAD_SIZE), BF16),
            buf((ROWS, heads), BF16),
            buf((ROWS, heads), BF16),
            buf((2, ROWS, 768), BF16),
            buf((PAIR, HEAD_SIZE), jnp.int32),
            buf((1, QROWS), jnp.int32),
            buf((1, QROWS), F32),
            buf((1, QROWS), F32),
            buf((HEAD_SIZE, QROWS), F32),
            buf((1, QROWS), F32),
            buf((1, QROWS), F32),
            buf((HEAD_SIZE, QROWS), F32),
            buf((NZ, 2, PAIR, HEAD_SIZE), BF16),
            buf((PAIR, HEAD_SIZE), F32),
            buf((PAIR, HEAD_SIZE), BF16),
            buf((PAIR, HEAD_SIZE), BF16),
            buf((ROWS, WIDTH), F32),
            buf((3, ROWS, WIDTH), BF16),
            buf((3, ROWS, WIDTH), BF16),
            buf((ROWS, WIDTH), F32),
            buf((3, ROWS, WIDTH), BF16),
            buf((3, ROWS, WIDTH), BF16),
            buf((2, 4, 2, PAIR, HEAD_SIZE), BF16),
            buf((2, 4, 2, PAIR, HEAD_SIZE), BF16),
            buf((2, 4, 2, 256, 256), BF16),
            buf((2, 4, 2, 256, 256), BF16),
            buf((2, 4, 3, 256, 256), BF16),
            buf((2, 4, 3, 256, 256), BF16),
            dma((5,)),
            dma((4, 3)),
            dma((4, 3)),
            dma((9,)),
            dma((9,)),
            dma((2, 2, 4)),
            dma((2, 2, 4)),
            dma((2, 4, 2)),
            dma((2, 4, 2)),
            dma((2, 4, 2)),
            dma((2, 4, 2)),
            dma((2, 4, 3)),
            dma((2, 4, 3)),
        ],
        compiler_params=pltpu.CompilerParams(
            collective_id=0, has_side_effects=True, vmem_limit_bytes=VMEM_LIMIT
        ),
    )(tok, up, wq, wo, freqs, exponents)


def settle_kernel(*refs):
    number = len(refs) // 2
    for i in range(number):
        refs[number + i][...] = refs[i][...]


def settle(*arrays):
    vmem = pl.BlockSpec(memory_space=pltpu.VMEM)
    return pl.pallas_call(
        settle_kernel,
        name="settle",
        out_shape=[jax.ShapeDtypeStruct(a.shape, a.dtype) for a in arrays],
        in_specs=[vmem] * len(arrays),
        out_specs=[vmem] * len(arrays),
        compiler_params=pltpu.CompilerParams(vmem_limit_bytes=VMEM_LIMIT),
    )(*arrays)


def local(tokens, input_projection_weight, w_out, upstream, exponents):
    half = HEAD_SIZE // 2
    freqs = jnp.power(F32(THETA), -jnp.arange(half, dtype=F32) * 2.0 / HEAD_SIZE)
    freqs = jnp.tile(freqs, 2).reshape(1, HEAD_SIZE)
    return settle(
        *layer(tokens, upstream, input_projection_weight, w_out, freqs, exponents)
    )


def solution(mesh):
    in_specs = (
        P(("dp", "seq"), "tensor"),
        P(None, "tensor"),
        P("tensor", None),
        P(("dp", "seq"), "tensor"),
        P("dp", "tensor"),
    )
    out_specs = (
        P(("dp", "seq"), "tensor"),
        P(("dp", "seq"), "tensor"),
        P(("dp", "seq"), "tensor"),
        P(("dp", "tensor"), "seq"),
    )
    return jax.shard_map(local, mesh=mesh, in_specs=in_specs, out_specs=out_specs, check_vma=False)
```

time: 175 us -> 137 us (0.78)
  Pallas kernels: 166 us -> 133 us
  local copies, waits for them, and re-layouts: 6.62 us -> 2.05 us
  other arithmetic: 1.95 us -> 0.01 us
    pallas_call x3 -> x2, Pallas kernels: 166 us -> 133 us  [the longest x1 131 us: layer(): pl.pallas_call(layer_kernel, name='layer', out_shape=[shape((ROWS, WIDTH)...]
    unnamed x8 -> x1, local copies, waits for them, and re-layouts: 5.05 us -> 1.46 us
where the time goes in v2:
time: 137 us; the launch traced here: 136 us
  Pallas kernels  133 us (97%)
  local copies, waits for them, and re-layouts  2.05 us (1%)
    pallas_call x1, Pallas kernels, layer(): pl.pallas_call(layer_kernel, name='layer', out_shape=[shape((ROWS, WIDTH)...  131 us

profile of v2, /device:TPU:2, one launch (start us, length us, event | category | flops | bytes accessed | tf_op | source)
XLA Modules:
  0.0 136.1 jit_solution(4820579710522562765)
XLA Ops:
  0.7 0.6 reshape_tile.3.freqs
  1.2 1.5 %copy.9.exponents = s32[192,6]{1,0:T(8,128)} copy(s32[192,6]{0,1:T(8,128)} %param.9) | data formatting | bytes 9216 | tf_op args[4]
  2.7 130.9 %layer.1 = (bf16[192,1024]{1,0:T(8,128)(2,1)}, bf16[192,1024]{1,0:T(8,128)(2,1)}, bf16[256,768]{1,0:T(8,128)(2,1)}, bf16[512,256]{1,0:T(8,128)(2,1)}) custom-call(bf16[192,1024]{1,0:T(8,128)(2,1)} %tok.1, bf16[192,1024]{1,0:T(8,128)(2,1)} %up.1, bf16[4096,768]{1,0:T(8,128)(2,1)} %wq_hbm.1, bf16[512,4096]{1,0:T(8,128)(2,1)} %wo_hbm.1, ...), custom_call_target="tpu_custom_call" | custom-call | tf_op jit(solution)/shard_map/layer/pallas_call | solution.py:491
  133.7 2.4 %settle.1 = (bf16[192,1024]{1,0:T(8,128)(2,1)}, bf16[192,1024]{1,0:T(8,128)(2,1)}, bf16[256,768]{1,0:T(8,128)(2,1)}, bf16[512,256]{1,0:T(8,128)(2,1)}) custom-call(bf16[192,1024]{1,0:T(8,128)(2,1)} %get-tuple-element.8.refs_0_, bf16[192,1024]{1,0:T(8,128)(2,1)} %get-tuple-element.9.refs_1_, bf16[256,768]{1,0:T(8,128)(2,1)} %get-tuple-element.10.refs_2_, ...), custom_call_target="tpu_custom_call" | custom-call | tf_op jit(solution)/shard_map/settle/pallas_call | solution.py:570
  (2 shorter events, 0.0 us)

commit v3 on v2

--- a/solution.py
+++ b/solution.py
@@ -3,6 +3,7 @@
 
 import jax
 import jax.numpy as jnp
+import numpy as np
 from jax import lax
 from jax.experimental import pallas as pl
 from jax.experimental.pallas import tpu as pltpu
@@ -50,10 +51,14 @@
     def xdev(self):
         return (self.d, (1 - self.xh) * NZ + self.z, self.t)
 
+    def diagonal(self, sign):
+        return (self.d, (1 - self.xh) * NZ + lax.rem(self.z + sign + NZ, NZ), self.t)
+
     def enter(self):
         barrier = pltpu.get_barrier_semaphore()
         partners = [self.tensor(1), self.tensor(2), self.tensor(3)]
         partners += [self.zdev(1), self.zdev(-1), self.xdev()]
+        partners += [self.diagonal(1), self.diagonal(-1)]
         for partner in partners:
             pl.semaphore_signal(barrier, inc=1, device_id=partner, device_id_type=MESH)
         pl.semaphore_wait(barrier, len(partners))
@@ -74,9 +79,7 @@
     return vectors * cosine + pltpu.roll(vectors, HEAD_SIZE // 2, 1) * sine
 
 
-def gather_column(place, kv, column, which, ss, rs, sends):
-    cut = pl.ds(pl.multiple_of(column * ROWS, ROWS), ROWS)
-
+def gather_column(place, kv, cut, which, ss, rs, sends, first=1):
     def part(step, di, z):
         z = lax.rem(z + 2 * NZ, NZ)
         return kv.at[di, z, cut] if step == 4 else kv.at[:, z, cut]
@@ -86,7 +89,7 @@
         sem = rs.at[which, di, step - 1]
         remote(ref, ref, ss.at[which, di, step - 1], sem, place.zdev(sign)).wait_recv()
 
-    for step in range(1, 5):
+    for step in range(first, 5):
         for di, sign in ((0, 1), (1, -1)):
             if step > 1:
                 arrived(step - 1, di, sign)
@@ -116,9 +119,9 @@
                 there = rbuf.at[di, step - 1, sub]
                 if step == 4:
                     here, there = here.at[cut], there.at[cut]
-                    here[...] = load(dest, sub, di).astype(BF16)
+                    here[...] = load(dest, sub, di, step, di).astype(BF16)
                 else:
-                    value = load(dest, sub, None)
+                    value = load(dest, sub, None, step, di)
                     before = rbuf.at[di, step, sub]
                     if step == 3:
                         before = before.at[cut]
@@ -140,7 +143,7 @@
                 sends.append(copy)
             yield
     for sub in subs:
-        total = load(place.z, sub, None)
+        total = load(place.z, sub, None, 0, 0)
         for di, sign in ((0, 1), (1, -1)):
             ref = rbuf.at[di, 0, sub]
             remote(ref, ref, ss.at[di, 0, sub], rs.at[di, 0, sub], place.zdev(sign)).wait_recv()
@@ -159,14 +162,15 @@
 
 def layer_kernel(
     tok, up, wq_hbm, wo_hbm, freqs, exponents,
-    attended, grad_tokens, gwq, gwo,
+    attended_hbm, grad_tokens_hbm, gwq_hbm, gwo_hbm,
     wq, wo, tok_all, up_all, tok_other, up_other, cosine, sine, expo,
     q, kv, do, merged, merged_other, gqkv,
     key_place, limit, top, total, acc, logsum, delta, dq,
-    dkv, kv_own, kv_out, kv_in,
+    dkv, dkv_other, kv_sum,
     att_own, att_s, att_r, tok_own, tok_s, tok_r,
     kv_sb, kv_rb, o_sb, o_rb, q_sb, q_rb,
-    load_sem, y_ss, y_rs, x_ss, x_rs, ag_ss, ag_rs,
+    attended, grad_tokens, gwq, gwo,
+    load_sem, store_sem, y_ss, y_rs, x_ss, x_rs, ag_ss, ag_rs,
     kv_ss, kv_rs, o_ss, o_rs, q_ss, q_rs,
 ):
     place = Place()
@@ -186,27 +190,96 @@
         copy.start()
         return copy
 
-    def spread(own, everyone, which):
-        copies = []
-        for offset in (1, 3, 2):
-            copy = remote(
-                own,
-                everyone.at[t],
-                y_ss.at[which, offset - 1],
-                y_rs.at[which, offset - 1],
-                place.tensor(offset),
-            )
+    def on_y(src, dst, which, i, offset):
+        return remote(src, dst, y_ss.at[which, i], y_rs.at[which, i], place.tensor(offset))
+
+    before, after, across = (lax.rem(t + i, NT) for i in (3, 1, 2))
+
+    def halves(first, rows):
+        return pl.ds(first, rows // 2), pl.ds(first + rows // 2, rows // 2)
+
+    def tensor_start(own, everyone, which, first=0, rows=ROWS):
+        part = pl.ds(first, rows)
+        for i, offset in ((0, 1), (1, 3)):
+            copy = on_y(own.at[part], everyone.at[t, part], which, i, offset)
             copy.start()
-            copies.append(copy)
-        return copies
-
-    def arrived(everyone, offset, which):
-        source = lax.rem(t + NT - offset, NT)
-        ref = everyone.at[source]
-        remote(
-            ref, ref, y_ss.at[which, offset - 1], y_rs.at[which, offset - 1], place.tensor(offset)
-        ).wait_recv()
-        return source
+            sends.append(copy)
+
+    def tensor_forward(everyone, which, first=0, rows=ROWS):
+        for i, offset, source in ((0, 1, before), (1, 3, after)):
+            ref = everyone.at[source, pl.ds(first, rows)]
+            on_y(ref, ref, which, i, offset).wait_recv()
+            ref = everyone.at[source, halves(first, rows)[i]]
+            copy = on_y(ref, ref, which, 2 + i, offset)
+            copy.start()
+            sends.append(copy)
+
+    def tensor_end(everyone, which, first=0, rows=ROWS):
+        for i, offset in ((0, 1), (1, 3)):
+            ref = everyone.at[across, halves(first, rows)[i]]
+            on_y(ref, ref, which, 2 + i, offset).wait_recv()
+
+    gives = lax.div(t, 2) == 1 - xh
+    holds = lax.div(t, 2) == xh
+    slot = lax.rem(t, 2)
+
+    def give(own, others, i):
+        @pl.when(gives)
+        def _():
+            remote(own, others.at[slot], x_ss.at[i], x_rs.at[i], place.xdev()).start()
+
+    def holder(source):
+        return lax.div(source, 2) == xh
+
+    def share_start(own, others, i, which):
+        @pl.when(holds)
+        def _():
+            ref = others.at[slot]
+            remote(own, ref, x_ss.at[i], x_rs.at[i], place.xdev()).wait_recv()
+            on_y(ref, ref, which, 0, 1).start()
+            on_y(ref, ref, which, 1, 3).start()
+
+    def share_forward(others, which):
+        for i, offset, source in ((0, 1, before), (1, 3, after)):
+
+            @pl.when(holder(source))
+            def _(i=i, offset=offset, source=source):
+                ref = others.at[lax.rem(source, 2)]
+                on_y(ref, ref, which, i, offset).wait_recv()
+                ref = others.at[lax.rem(source, 2), halves(0, ROWS)[i]]
+                on_y(ref, ref, which, 2 + i, offset).start()
+
+    def share_end(others, which):
+        @pl.when(holder(across))
+        def _():
+            for i, offset in ((0, 1), (1, 3)):
+                ref = others.at[lax.rem(across, 2), halves(0, ROWS)[i]]
+                on_y(ref, ref, which, 2 + i, offset).wait_recv()
+
+    def share_sent(own, others, i, which):
+        @pl.when(gives)
+        def _():
+            remote(own, others.at[slot], x_ss.at[i], x_rs.at[i], place.xdev()).wait_send()
+
+        @pl.when(holds)
+        def _():
+            ref = others.at[slot]
+            on_y(ref, ref, which, 0, 1).wait_send()
+            on_y(ref, ref, which, 1, 3).wait_send()
+
+        for i, offset, source in ((0, 1, before), (1, 3, after)):
+
+            @pl.when(holder(source))
+            def _(i=i, offset=offset, source=source):
+                ref = others.at[lax.rem(source, 2), halves(0, ROWS)[i]]
+                on_y(ref, ref, which, 2 + i, offset).wait_send()
+
+    stores = []
+
+    def store(src, dst):
+        copy = pltpu.make_async_copy(src, dst, store_sem.at[len(stores)])
+        copy.start()
+        stores.append(copy)
 
     def scatter_tensor(term, own, sbuf, rbuf, which):
         for offset in (1, 3, 2):
@@ -236,7 +309,9 @@
             value = value + ref[...]
         out[...] = value.astype(BF16)
 
-    token_sends = spread(tok, tok_all, 0)
+    half = ROWS // 2
+    tensor_start(tok, tok_all, 0, 0, half)
+    give(up, up_other, 2)
     tok_all[t] = tok[...]
     up_all[t] = up[...]
     position = lax.broadcasted_iota(jnp.int32, (ROWS, HEAD_SIZE), 0) + place.s * ROWS
@@ -245,11 +320,11 @@
     low = lax.broadcasted_iota(jnp.int32, (ROWS, HEAD_SIZE), 1) < HEAD_SIZE // 2
     sines = jnp.sin(angles)
     sine[...] = jnp.where(low, -sines, sines)
-    groups = exponents.shape[0]
+    groups = exponents.shape[1]
     group = lax.broadcasted_iota(jnp.int32, (ROWS, groups), 0) // SCALE_TOKENS
     group = group + place.s * (ROWS // SCALE_TOKENS)
     pick = lax.broadcasted_iota(jnp.int32, (ROWS, groups), 1) == group
-    expo[...] = dot(pick.astype(F32).astype(BF16), exponents[...].astype(F32).astype(BF16), 1, 0)
+    expo[...] = dot(pick.astype(F32).astype(BF16), exponents[...].astype(F32).astype(BF16), 1, 1)
     row = lax.broadcasted_iota(jnp.int32, (PAIR, HEAD_SIZE), 0)
     key_place[...] = jnp.where(row < ROWS, row, row + (NZ - 1) * ROWS)
     limit[...] = place.s * ROWS + lax.rem(
@@ -259,37 +334,18 @@
     total[...] = jnp.zeros(total.shape, F32)
     acc[...] = jnp.zeros(acc.shape, F32)
     dq[...] = jnp.zeros(dq.shape, F32)
-    loads[0].wait()
-    projected = dot(tok[...], wq[pl.ds(pl.multiple_of(t * WIDTH, WIDTH), WIDTH)], 1, 0)
-    for load in loads[1:]:
-        load.wait()
-    for offset in (1, 3, 2):
-        source = arrived(tok_all, offset, 0)
-        rows = pl.ds(pl.multiple_of(source * WIDTH, WIDTH), WIDTH)
-        if offset == 2:
-            for copy in token_sends:
-                copy.wait_send()
-            sends.extend(spread(up, up_all, 1))
-        projected = projected + dot(tok_all[source], wq[rows], 1, 0)
-
-    c, s = cosine[...], sine[...]
-    mine = pl.ds(pl.multiple_of(xh * ROWS, ROWS), ROWS)
-    kv[0, z, mine] = turn(projected[:, 512:640], c, s).astype(BF16)
-    kv[1, z, mine] = projected[:, 640:768].astype(BF16)
-    x_kv = swap(kv.at[:, z, mine], kv.at[:, z, mine], 0)
-    own_ring = gather_column(place, kv, xh, 0, ag_ss, ag_rs, sends)
-    run(own_ring, 1)
-    for h in range(QUERY_PER_KEY):
-        q[pl.ds(h * ROWS, ROWS)] = turn(
-            projected[:, h * HEAD_SIZE : (h + 1) * HEAD_SIZE], c, s
-        ).astype(BF16)
-    theirs = pl.ds(pl.multiple_of((1 - xh) * ROWS, ROWS), ROWS)
-    other = kv.at[:, z, theirs]
-    remote(other, other, x_ss.at[0], x_rs.at[0], place.xdev()).wait_recv()
-    sends.append(x_kv)
-    other_ring = gather_column(place, kv, 1 - xh, 1, ag_ss, ag_rs, sends)
-    run(other_ring, 1)
-    x_tok = [swap(tok_all.at[2 * (1 - xh)], tok_other.at[0], 1)]
+    def weight_rows(source):
+        return pl.ds(pl.multiple_of(source * WIDTH, WIDTH), WIDTH)
+
+    def project_kv(first, sources):
+        part = pl.ds(first, half)
+        return sum(
+            dot(tok_all[source, part], wq[weight_rows(source), 512:768], 1, 0)
+            for source in sources
+        )
+
+    def project_q(source):
+        return dot(tok_all[source], wq[weight_rows(source), 0:512], 1, 0)
 
     def around(step):
         return lax.rem(z + step + NZ, NZ)
@@ -311,48 +367,107 @@
             acc[:, cut] = acc[:, cut] * alpha + dot(values, weights.astype(BF16), 0, 0)
 
     def merged_term(source):
-        columns = pl.ds(pl.multiple_of(source * WIDTH, WIDTH), WIDTH)
-        return dot(up_all[source], wo[:, columns], 1, 1)
-
-    def step_rings():
-        run(own_ring, 1)
-        run(other_ring, 1)
-
+        return dot(up_all[source], wo[:, weight_rows(source)], 1, 1)
+
+    c, s = cosine[...], sine[...]
+    own_rings, other_rings, x_kv = [], [], []
+
+    def column_part(column, first):
+        return pl.ds(pl.multiple_of(column * ROWS + first, half), half)
+
+    def send_kv(i, projected):
+        first = i * half
+        part = slice(first, first + half)
+        rows = column_part(xh, first)
+        kv[0, z, rows] = turn(projected[:, 0:128], c[part], s[part]).astype(BF16)
+        kv[1, z, rows] = projected[:, 128:256].astype(BF16)
+        x_kv.append(swap(kv.at[:, z, rows], kv.at[:, z, rows], (0, 14)[i]))
+        own_rings.append(gather_column(place, kv, rows, i, ag_ss, ag_rs, sends))
+        run(own_rings[i], 1)
+        for di, sign in ((0, 1), (1, -1)):
+            ref = kv.at[:, z, rows]
+            copy = remote(
+                ref, ref, ag_ss.at[2 + i, di, 0], ag_rs.at[2 + i, di, 0], place.diagonal(sign)
+            )
+            copy.start()
+            sends.append(copy)
+        other = column_part(1 - xh, first)
+        other_rings.append(gather_column(place, kv, other, 2 + i, ag_ss, ag_rs, sends, 2))
+
+    def receive_kv(i):
+        rows = column_part(1 - xh, i * half)
+        ref = kv.at[:, z, rows]
+        sem = (0, 14)[i]
+        remote(ref, ref, x_ss.at[sem], x_rs.at[sem], place.xdev()).wait_recv()
+        sends.append(x_kv[i])
+
+    for load in loads:
+        load.wait()
+    tensor_forward(tok_all, 0, 0, half)
+    tensor_start(tok, tok_all, 6, half, half)
+    projected = project_kv(0, (t, before, after))
+    tensor_end(tok_all, 0, 0, half)
+    send_kv(0, projected + project_kv(0, (across,)))
+    tensor_forward(tok_all, 6, half, half)
+    projected = project_kv(half, (t, before, after))
+    run(own_rings[0], 1)
+    run(other_rings[0], 1)
+    tensor_end(tok_all, 6, half, half)
+    tensor_start(up, up_all, 1)
+    send_kv(1, projected + project_kv(half, (across,)))
+    run(own_rings[0], 1)
+    run(other_rings[0], 1)
+    projected = project_q(t) + project_q(before) + project_q(after) + project_q(across)
+    for h in range(QUERY_PER_KEY):
+        q[pl.ds(h * ROWS, ROWS)] = turn(
+            projected[:, h * HEAD_SIZE : (h + 1) * HEAD_SIZE], c, s
+        ).astype(BF16)
+    share_start(up, up_other, 2, 2)
+    run(own_rings[1], 1)
+    run(other_rings[1], 1)
+    receive_kv(0)
+    receive_kv(1)
+    give(tok, tok_other, 1)
     forward(z)
-    step_rings()
+    run(own_rings[0], 1)
+    run(other_rings[0], 1)
+    run(own_rings[1], 1)
+    run(other_rings[1], 1)
+    run(own_rings[0])
+    run(other_rings[0])
     forward(around(1))
     forward(around(-1))
-    load_wo.wait()
-    step_rings()
+    run(own_rings[1], 1)
+    run(other_rings[1], 1)
     forward(around(2))
     forward(around(-2))
-    grad = merged_term(t)
-    grad = grad + merged_term(arrived(up_all, 1, 1))
-    step_rings()
+    tensor_forward(up_all, 1)
+    load_wo.wait()
     forward(around(3))
     forward(around(-3))
-    grad = grad + merged_term(arrived(up_all, 3, 1))
-    grad = grad + merged_term(arrived(up_all, 2, 1))
-    x_up = [swap(up_all.at[2 * (1 - xh) + i], up_other.at[i], 2 + i) for i in range(2)]
-    for h in range(QUERY_PER_KEY):
-        do[pl.ds(h * ROWS, ROWS)] = grad[:, h * HEAD_SIZE : (h + 1) * HEAD_SIZE].astype(BF16)
-    run(own_ring)
-    run(other_ring)
+    share_forward(up_other, 2)
+    run(own_rings[1])
+    run(other_rings[1])
     forward(around(4))
 
     out_t = (acc[...] / total[...]).astype(BF16)
     out = out_t.astype(F32).T.astype(BF16)
     for h in range(QUERY_PER_KEY):
         merged[:, h * HEAD_SIZE : (h + 1) * HEAD_SIZE] = out[h * ROWS : (h + 1) * ROWS]
-    x_merged = swap(merged, merged_other, 4)
+    x_merged = []
+    for i, sem in enumerate((3, 15)):
+        ref = pl.ds(i * 256, 256)
+        x_merged.append(swap(merged.at[:, ref], merged_other.at[:, ref], sem))
+    tensor_end(up_all, 1)
+    grad = merged_term(t) + merged_term(before) + merged_term(after) + merged_term(across)
+    for h in range(QUERY_PER_KEY):
+        do[pl.ds(h * ROWS, ROWS)] = grad[:, h * HEAD_SIZE : (h + 1) * HEAD_SIZE].astype(BF16)
     logsum[...] = top[...] * SCALE2 + jnp.log2(total[...])
     delta[...] = jnp.sum(do[...].astype(F32).T * out_t.astype(F32), axis=0, keepdims=True)
 
-    def backward(zk):
+    def backward(slot, zk):
         keys = kv[0, zk]
         values = kv[1, zk]
-        dk = jnp.zeros((PAIR, HEAD_SIZE), F32)
-        dv = jnp.zeros((PAIR, HEAD_SIZE), F32)
         scores = dot(keys, q[...], 1, 1)
         allowed = key_place[:, 0:1] <= limit[...] - zk * ROWS
         probs = jnp.exp2(jnp.where(allowed, scores * SCALE2 - logsum[...], -jnp.inf))
@@ -363,61 +478,37 @@
         dq[...] += dot(keys, grad_scores, 0, 0)
         for column in range(2):
             rows = slice(column * ROWS, (column + 1) * ROWS)
-            dkv[zk, column, 0:ROWS] = dk[rows]
-            dkv[zk, column, ROWS:PAIR] = dv[rows]
-
-    def load_kv(dest, sub, part):
-        ref = dkv.at[dest, (1 - xh) if sub == 0 else xh]
+            dkv[slot, column, 0:ROWS] = dk[rows]
+            dkv[slot, column, ROWS:PAIR] = dv[rows]
+        sends.append(swap(dkv.at[slot, 1 - xh], dkv_other.at[slot], 6 + slot))
+
+    kv_here = set()
+
+    def load_kv(dest, sub, part, step, di):
+        slot = {4: 0, 3: 1, 2: 3, 1: 5, 0: 7}[step] + (di if step in (1, 2, 3) else 0)
+        ref = dkv_other.at[slot]
+        if slot not in kv_here:
+            kv_here.add(slot)
+            remote(ref, ref, x_ss.at[6 + slot], x_rs.at[6 + slot], place.xdev()).wait_recv()
+        rows = pl.ds(sub * ROWS, ROWS)
         if part is not None:
-            return ref[pl.ds(part * ROWS, ROWS)].astype(F32)
-        return ref[...].astype(F32)
+            rows = pl.ds(sub * ROWS + part * (ROWS // 2), ROWS // 2)
+        return dkv[slot, xh, rows].astype(F32) + ref[rows].astype(F32)
 
     def done_kv(sub, value):
-        if sub == 0:
-            kv_out[...] = value.astype(BF16)
-        else:
-            kv_own[...] = value
+        kv_sum[pl.ds(sub * ROWS, ROWS)] = value
 
     ring_kv = scatter_ring(
-        place, (0, 1), PAIR, load_kv, kv_sb, kv_rb, kv_ss, kv_rs, sends, done_kv
+        place, (0, 1), ROWS, load_kv, kv_sb, kv_rb, kv_ss, kv_rs, sends, done_kv
     )
 
     def attended_term(dest):
         return dot(merged[...], wo[:, pl.ds(pl.multiple_of(dest * WIDTH, WIDTH), WIDTH)], 1, 0)
 
-    backward(around(4))
-    run(ring_kv, 2)
-    scatter_tensor(attended_term, att_own, att_s, att_r, 2)
-    backward(around(3))
-    backward(around(-3))
-    run(ring_kv, 2)
-    backward(around(2))
-    backward(around(-2))
-    run(ring_kv, 2)
-    backward(around(1))
-    backward(around(-1))
-    run(ring_kv, 2)
-    backward(z)
-
-    def squeeze(value, column):
-        e = expo[:, column : column + 1]
-        sent = jnp.clip(value * jnp.exp2(-e), -127.0, 127.0).astype(BF16)
-        return sent.astype(F32) * jnp.exp2(e)
-
-    grad = dq[...].T * SCALE
-    for h in range(QUERY_PER_KEY):
-        gqkv[0, :, h * HEAD_SIZE : (h + 1) * HEAD_SIZE] = turn(
-            squeeze(grad[h * ROWS : (h + 1) * ROWS], h), c, -s
-        ).astype(BF16)
-    x_gq = swap(gqkv.at[0, :, pl.ds(0, 512)], gqkv.at[1, :, pl.ds(0, 512)], 5)
-    x_tok.append(swap(tok_all.at[2 * (1 - xh) + 1], tok_other.at[1], 6))
-    run(ring_kv)
-    x_dkv = swap(kv_out, kv_in, 7)
-
     def columns(dest):
         return pl.ds(pl.multiple_of(lax.rem(dest, 4) * 256, 256), 256)
 
-    def load_o(dest, sub, part):
+    def load_o(dest, sub, part, step, di):
         first = sub * 256 + (0 if part is None else part * 128)
         last = first + (256 if part is None else 128)
         shard = lax.div(dest, 4)
@@ -429,7 +520,7 @@
     def done_o(sub, value):
         gwo[pl.ds(sub * 256, 256)] = value.astype(BF16)
 
-    def load_q(dest, sub, part):
+    def load_q(dest, sub, part, step, di):
         shard = lax.div(dest, 4)
         left = tok_all[2 * xh + shard, :, columns(dest)]
         left_other = tok_other[shard, :, columns(dest)]
@@ -440,45 +531,82 @@
         return dot(left, gqkv[0, :, cut], 0, 0) + dot(left_other, gqkv[1, :, cut], 0, 0)
 
     def done_q(sub, value):
-        gwq[:, sub * 256 : (sub + 1) * 256] = value.astype(BF16)
+        cut = pl.ds(sub * 256, 256)
+        gwq[sub] = value.astype(BF16)
+        store(gwq.at[sub], gwq_hbm.at[:, cut])
 
     ring_o = scatter_ring(place, (0, 1), 256, load_o, o_sb, o_rb, o_ss, o_rs, sends, done_o)
     ring_q = scatter_ring(place, (0, 1), 256, load_q, q_sb, q_rb, q_ss, q_rs, sends, done_q)
     ring_k = scatter_ring(place, (2,), 256, load_q, q_sb, q_rb, q_ss, q_rs, sends, done_q)
-    for copy in x_up:
-        copy.wait()
-    x_merged.wait()
-    run(ring_o, 4)
-    x_dkv.wait()
-    grad = kv_own[...] + kv_in[...]
-    gqkv[0, :, 512:640] = turn(squeeze(grad[:ROWS], 4), c, -s).astype(BF16)
-    gqkv[0, :, 640:768] = squeeze(grad[ROWS:], 5).astype(BF16)
-    x_gkv = swap(gqkv.at[0, :, pl.ds(512, 256)], gqkv.at[1, :, pl.ds(512, 256)], 8)
+
+    def squeeze(value, column):
+        e = expo[:, column : column + 1]
+        sent = jnp.clip(value * jnp.exp2(-e), -127.0, 127.0).astype(BF16)
+        return sent.astype(F32) * jnp.exp2(e)
+
+    share_start(tok, tok_other, 1, 3)
+    backward(0, around(4))
+    backward(1, around(3))
+    backward(2, around(-3))
+    x_merged[0].wait()
+    share_end(up_other, 2)
+    run(ring_o, 1)
+    x_merged[1].wait()
+    run(ring_o, 1)
+    backward(3, around(2))
+    backward(4, around(-2))
+    run(ring_kv, 2)
     run(ring_o, 2)
+    share_forward(tok_other, 3)
+    backward(5, around(1))
+    backward(6, around(-1))
+    backward(7, z)
+    run(ring_kv, 2)
+    grad = dq[...].T * SCALE
+    for h in range(QUERY_PER_KEY):
+        gqkv[0, :, h * HEAD_SIZE : (h + 1) * HEAD_SIZE] = turn(
+            squeeze(grad[h * ROWS : (h + 1) * ROWS], h), c, -s
+        ).astype(BF16)
+    x_gq = swap(gqkv.at[0, :, pl.ds(0, 512)], gqkv.at[1, :, pl.ds(0, 512)], 4)
+    run(ring_o, 2)
+    scatter_tensor(attended_term, att_own, att_s, att_r, 4)
+    run(ring_kv, 2)
+    run(ring_o, 2)
+    run(ring_kv, 2)
+    x_gq.wait()
+    share_end(tok_other, 3)
+    run(ring_q, 2)
+    run(ring_kv)
+    gqkv[0, :, 512:640] = turn(squeeze(kv_sum[0:ROWS], 4), c, -s).astype(BF16)
+    gqkv[0, :, 640:768] = squeeze(kv_sum[ROWS:PAIR], 5).astype(BF16)
+    x_gkv = swap(gqkv.at[0, :, pl.ds(512, 256)], gqkv.at[1, :, pl.ds(512, 256)], 5)
+    run(ring_o)
+    store(gwo, gwo_hbm)
+    run(ring_q, 2)
 
     def tokens_term(dest):
         return dot(gqkv[0], wq[pl.ds(pl.multiple_of(dest * WIDTH, WIDTH), WIDTH)], 1, 1)
 
-    scatter_tensor(tokens_term, tok_own, tok_s, tok_r, 3)
-    run(ring_o, 2)
-    x_gq.wait()
-    for copy in x_tok:
-        copy.wait()
-    run(ring_q, 2)
-    run(ring_o)
-    collect_tensor(att_own, att_r, 2, attended)
-    run(ring_q, 2)
     x_gkv.wait()
+    run(ring_k, 1)
+    scatter_tensor(tokens_term, tok_own, tok_s, tok_r, 5)
     run(ring_k, 1)
     run(ring_q, 2)
     run(ring_k, 1)
-    collect_tensor(tok_own, tok_r, 3, grad_tokens)
+    collect_tensor(att_own, att_r, 4, attended)
+    store(attended, attended_hbm)
     run(ring_q, 2)
-    run(ring_k, 2)
+    run(ring_k, 1)
+    collect_tensor(tok_own, tok_r, 5, grad_tokens)
+    store(grad_tokens, grad_tokens_hbm)
     run(ring_q)
     run(ring_k)
+    share_sent(up, up_other, 2, 2)
+    share_sent(tok, tok_other, 1, 3)
     for copy in sends:
         copy.wait_send()
+    for copy in stores:
+        copy.wait()
 
 
 def layer(tok, up, wq, wo, freqs, exponents):
@@ -498,7 +626,7 @@
             shape((512, 256), BF16),
         ],
         in_specs=[vmem, vmem, hbm, hbm, vmem, vmem],
-        out_specs=[vmem] * 4,
+        out_specs=[hbm] * 4,
         scratch_shapes=[
             buf(wq.shape, BF16),
             buf(wo.shape, BF16),
@@ -524,28 +652,32 @@
             buf((1, QROWS), F32),
             buf((HEAD_SIZE, QROWS), F32),
             buf((NZ, 2, PAIR, HEAD_SIZE), BF16),
+            buf((NZ, PAIR, HEAD_SIZE), BF16),
             buf((PAIR, HEAD_SIZE), F32),
-            buf((PAIR, HEAD_SIZE), BF16),
-            buf((PAIR, HEAD_SIZE), BF16),
             buf((ROWS, WIDTH), F32),
             buf((3, ROWS, WIDTH), BF16),
             buf((3, ROWS, WIDTH), BF16),
             buf((ROWS, WIDTH), F32),
             buf((3, ROWS, WIDTH), BF16),
             buf((3, ROWS, WIDTH), BF16),
-            buf((2, 4, 2, PAIR, HEAD_SIZE), BF16),
-            buf((2, 4, 2, PAIR, HEAD_SIZE), BF16),
+            buf((2, 4, 2, ROWS, HEAD_SIZE), BF16),
+            buf((2, 4, 2, ROWS, HEAD_SIZE), BF16),
             buf((2, 4, 2, 256, 256), BF16),
             buf((2, 4, 2, 256, 256), BF16),
             buf((2, 4, 3, 256, 256), BF16),
             buf((2, 4, 3, 256, 256), BF16),
+            buf((ROWS, WIDTH), BF16),
+            buf((ROWS, WIDTH), BF16),
+            buf((3, 256, 256), BF16),
+            buf((512, 256), BF16),
             dma((5,)),
-            dma((4, 3)),
-            dma((4, 3)),
-            dma((9,)),
-            dma((9,)),
-            dma((2, 2, 4)),
-            dma((2, 2, 4)),
+            dma((6,)),
+            dma((7, 4)),
+            dma((7, 4)),
+            dma((16,)),
+            dma((16,)),
+            dma((4, 2, 4)),
+            dma((4, 2, 4)),
             dma((2, 4, 2)),
             dma((2, 4, 2)),
             dma((2, 4, 2)),
@@ -579,10 +711,10 @@
 
 def local(tokens, input_projection_weight, w_out, upstream, exponents):
     half = HEAD_SIZE // 2
-    freqs = jnp.power(F32(THETA), -jnp.arange(half, dtype=F32) * 2.0 / HEAD_SIZE)
-    freqs = jnp.tile(freqs, 2).reshape(1, HEAD_SIZE)
+    freqs = np.power(np.float32(THETA), -np.arange(half, dtype=np.float32) * 2.0 / HEAD_SIZE)
+    freqs = jnp.asarray(np.tile(freqs, 2).reshape(1, HEAD_SIZE), F32)
     return settle(
-        *layer(tokens, upstream, input_projection_weight, w_out, freqs, exponents)
+        *layer(tokens, upstream, input_projection_weight, w_out, freqs, exponents.T)
     )
 
 

time: 137 us -> 120 us (0.88)
  Pallas kernels: 133 us -> 117 us
  local copies, waits for them, and re-layouts: 2.05 us -> 0 us
    pallas_call x1, Pallas kernels: 131 us -> 115 us  [layer(): pl.pallas_call(layer_kernel, name='layer', out_shape=[shape((ROWS, WIDTH)...]
    unnamed x1 -> x0, local copies, waits for them, and re-layouts: 1.46 us -> none
where the time goes in v3:
time: 120 us; the launch traced here: 118 us
  Pallas kernels  117 us (98%)
    pallas_call x1, Pallas kernels, layer(): pl.pallas_call(layer_kernel, name='layer', out_shape=[shape((ROWS, WIDTH)...  115 us
    pallas_call x1, Pallas kernels, settle(): pl.pallas_call(settle_kernel, name='settle', out_shape=[jax.ShapeDtypeStr...  2.43 us

profile of v3, /device:TPU:2, one launch (start us, length us, event | category | flops | bytes accessed | tf_op | source)
XLA Modules:
  0.0 117.9 jit_solution(1522529270575278564)
XLA Ops:
  0.6 114.8 %layer.1 = (bf16[192,1024]{1,0:T(8,128)(2,1)}, bf16[192,1024]{1,0:T(8,128)(2,1)}, bf16[256,768]{1,0:T(8,128)(2,1)}, bf16[512,256]{1,0:T(8,128)(2,1)}) custom-call(bf16[192,1024]{1,0:T(8,128)(2,1)} %tok.1, bf16[192,1024]{1,0:T(8,128)(2,1)} %up.1, bf16[4096,768]{1,0:T(8,128)(2,1)} %wq_hbm.1, bf16[512,4096]{1,0:T(8,128)(2,1)} %wo_hbm.1, ...), custom_call_target="tpu_custom_call" | custom-call | tf_op jit(solution)/shard_map/layer/pallas_call | solution.py:619
  115.5 2.4 %settle.1 = (bf16[192,1024]{1,0:T(8,128)(2,1)}, bf16[192,1024]{1,0:T(8,128)(2,1)}, bf16[256,768]{1,0:T(8,128)(2,1)}, bf16[512,256]{1,0:T(8,128)(2,1)}) custom-call(bf16[192,1024]{1,0:T(8,128)(2,1)} %get-tuple-element.8.refs_0_, bf16[192,1024]{1,0:T(8,128)(2,1)} %get-tuple-element.9.refs_1_, bf16[256,768]{1,0:T(8,128)(2,1)} %get-tuple-element.10.refs_2_, ...), custom_call_target="tpu_custom_call" | custom-call | tf_op jit(solution)/shard_map/settle/pallas_call | solution.py:702

commit v4 on v3

v4 whole, which is shorter than its diff:
```python
import functools
import math

import jax
import jax.numpy as jnp
import numpy as np
from jax import lax
from jax.experimental import pallas as pl
from jax.experimental.pallas import tpu as pltpu
from jax.sharding import PartitionSpec as P

HEAD_SIZE = 128
QUERY_PER_KEY = 4
SCALE_TOKENS = 16
THETA = 500000.0

NZ = 8
NT = 4
ROWS = 192
QROWS = QUERY_PER_KEY * ROWS
PAIR = 2 * ROWS
WIDTH = 1024
MESH = pl.DeviceIdType.MESH
BF16 = jnp.bfloat16
F32 = jnp.float32
SCALE = 1.0 / math.sqrt(HEAD_SIZE)
SCALE2 = SCALE * math.log2(math.e)
VMEM_LIMIT = 60 * 2**20


def dot(left, right, left_dim, right_dim):
    return lax.dot_general(
        left, right, (((left_dim,), (right_dim,)), ((), ())), preferred_element_type=F32
    )


class Place:
    def __init__(self):
        self.d = lax.axis_index("dp")
        self.s = lax.axis_index("seq")
        self.t = lax.axis_index("tensor")
        self.xh = lax.div(self.s, NZ)
        self.z = lax.rem(self.s, NZ)

    def tensor(self, offset):
        return (self.d, self.s, lax.rem(self.t + offset, NT))

    def zdev(self, sign):
        return (self.d, self.xh * NZ + lax.rem(self.z + sign + NZ, NZ), self.t)

    def xdev(self):
        return (self.d, (1 - self.xh) * NZ + self.z, self.t)

    def diagonal(self, sign):
        return (self.d, (1 - self.xh) * NZ + lax.rem(self.z + sign + NZ, NZ), self.t)

    def enter(self):
        barrier = pltpu.get_barrier_semaphore()
        partners = [self.tensor(1), self.tensor(2), self.tensor(3)]
        partners += [self.zdev(i) for i in range(1, NZ)] + [self.xdev()]
        partners += [self.diagonal(1), self.diagonal(-1)]
        for partner in partners:
            pl.semaphore_signal(barrier, inc=1, device_id=partner, device_id_type=MESH)
        pl.semaphore_wait(barrier, len(partners))


def remote(src, dst, send_sem, recv_sem, device):
    return pltpu.make_async_remote_copy(
        src_ref=src,
        dst_ref=dst,
        send_sem=send_sem,
        recv_sem=recv_sem,
        device_id=device,
        device_id_type=MESH,
    )


def turn(vectors, cosine, sine):
    return vectors * cosine + pltpu.roll(vectors, HEAD_SIZE // 2, 1) * sine


def gather_ring(place, part, which, ss, rs, sends, first=1):
    def arrived(step, di, sign):
        ref = part(step, di, place.z - sign * step)
        sem = rs.at[which, di, step - 1]
        remote(ref, ref, ss.at[0], sem, place.zdev(sign)).wait_recv()

    for step in range(first, 5):
        for di, sign in ((0, 1), (1, -1)):
            if step > 1:
                arrived(step - 1, di, sign)
            ref = part(step, di, place.z - sign * (step - 1))
            copy = remote(
                ref,
                ref,
                ss.at[0],
                rs.at[which, di, step - 1],
                place.zdev(sign),
            )
            copy.start()
            sends.append(copy)
        yield
    for di, sign in ((0, 1), (1, -1)):
        arrived(4, di, sign)


def scatter_ring(place, subs, rows, load, sbuf, rbuf, ss, rs, sends, done):
    half = rows // 2
    for step in (4, 3, 2, 1):
        for sub in subs:
            for di, sign in ((0, 1), (1, -1)):
                dest = lax.rem(place.z + sign * step + NZ, NZ)
                cut = pl.ds(di * half, half)
                here = sbuf.at[di, step - 1, sub]
                there = rbuf.at[di, step - 1, sub]
                if step == 4:
                    here, there = here.at[cut], there.at[cut]
                    here[...] = load(dest, sub, di, step, di).astype(BF16)
                else:
                    value = load(dest, sub, None, step, di)
                    before = rbuf.at[di, step, sub]
                    if step == 3:
                        before = before.at[cut]
                    remote(
                        before, before, ss.at[0], rs.at[di, step, sub], place.zdev(sign)
                    ).wait_recv()
                    if step == 3:
                        here[cut] = (value[di * half : (di + 1) * half] + before[...]).astype(BF16)
                        rest = 1 - di
                        here[pl.ds(rest * half, half)] = value[
                            rest * half : (rest + 1) * half
                        ].astype(BF16)
                    else:
                        here[...] = (value + before[...]).astype(BF16)
                copy = remote(
                    here, there, ss.at[0], rs.at[di, step - 1, sub], place.zdev(sign)
                )
                copy.start()
                sends.append(copy)
            yield
    for sub in subs:
        total = load(place.z, sub, None, 0, 0)
        for di, sign in ((0, 1), (1, -1)):
            ref = rbuf.at[di, 0, sub]
            remote(ref, ref, ss.at[0], rs.at[di, 0, sub], place.zdev(sign)).wait_recv()
            total = total + ref[...]
        done(sub, total)


def run(steps, count=None):
    if count is None:
        for _ in steps:
            pass
    else:
        for _ in range(count):
            next(steps)


class TwoStages:
    def __init__(self, place, rows, term, sbuf, rbuf, ss, rs, sends):
        self.place, self.half, self.term, self.sends = place, rows // 2, term, sends
        self.refs = sbuf, rbuf, ss, rs

    def copy(self, di, step, hops):
        sbuf, rbuf, ss, rs = self.refs
        at = (di, step - 1)
        here, there = sbuf.at[at], rbuf.at[at]
        if step == 4:
            cut = pl.ds(di * self.half, self.half)
            here, there = here.at[cut], there.at[cut]
        return remote(here, there, ss.at[0], rs.at[at], self.place.zdev(hops))

    def send(self, di, step, hops, value):
        sbuf = self.refs[0]
        if step == 4:
            cut = slice(di * self.half, (di + 1) * self.half)
            sbuf[di, step - 1, cut] = value[cut].astype(BF16)
        else:
            sbuf[di, step - 1] = value.astype(BF16)
        copy = self.copy(di, step, hops)
        copy.start()
        self.sends.append(copy)

    def far(self):
        value = self.term(4, 0)
        for di, sign in ((0, 1), (1, -1)):
            self.send(di, 3, sign, self.term(3, di))
            self.send(di, 4, 2 * sign, value)

    def near(self):
        for di, sign in ((0, 1), (1, -1)):
            self.send(di, 1, sign, self.term(1, di))

    def middle(self):
        half, (_, rbuf, _, _) = self.half, self.refs
        for di, sign in ((0, 1), (1, -1)):
            value = self.term(2, di)
            self.copy(di, 3, sign).wait_recv()
            self.copy(di, 4, 2 * sign).wait_recv()
            value = value + rbuf[di, 2]
            parts = [value[:half], value[half:]]
            parts[di] = parts[di] + rbuf[di, 3, di * half : (di + 1) * half]
            self.send(di, 2, 2 * sign, jnp.concatenate(parts, axis=0))

    def end(self):
        value = self.term(0, 0)
        for di, sign in ((0, 1), (1, -1)):
            for step in (1, 2):
                self.copy(di, step, step * sign).wait_recv()
                value = value + self.refs[1][di, step - 1]
        return value


def layer_kernel(
    tok_hbm, up_hbm, wq_hbm, wo_hbm, freqs, exponents,
    attended_hbm, grad_tokens_hbm, gwq_hbm, gwo_hbm,
    wq, wo, tok_all, up_all, tok_other, slab, cosine, sine, expo,
    q, kv, do, merged, merged_all, gqkv,
    key_place, limit, top, total, acc, logsum, delta, dq,
    dkv, dkv_other,
    att_own, att_s, att_r, tok_own, tok_s, tok_r,
    kv_sb, kv_rb, o_sb, o_rb, q_sb, q_rb, k_sb, k_rb,
    attended, grad_tokens, gwq, gwo,
    load_sem, store_sem, send_sem, y_rs, x_rs, ag_rs,
    kv_rs, m_rs, a_rs, q_rs, k_rs,
):
    place = Place()
    t, xh, z = place.t, place.xh, place.z
    tok, up = tok_all.at[t], up_all.at[t]
    load_tok = pltpu.make_async_copy(tok_hbm, tok, load_sem.at[5])
    load_tok.start()
    load_up = pltpu.make_async_copy(up_hbm, up, load_sem.at[6])
    load_up.start()
    loads = []
    for i in range(NT):
        rows = pl.ds(pl.multiple_of(lax.rem(t + (0, 1, 3, 2)[i], NT) * WIDTH, WIDTH), WIDTH)
        loads.append(pltpu.make_async_copy(wq_hbm.at[rows], wq.at[rows], load_sem.at[i]))
        loads[-1].start()
    load_wo = pltpu.make_async_copy(wo_hbm, wo, load_sem.at[4])
    load_wo.start()
    place.enter()
    sends = []
    half = ROWS // 2

    def swap(src, dst, i):
        copy = remote(src, dst, send_sem.at[0], x_rs.at[i], place.xdev())
        copy.start()
        sends.append(copy)
        return copy

    def on_y(src, dst, which, i, offset):
        return remote(src, dst, send_sem.at[0], y_rs.at[which, i], place.tensor(offset))

    before, after, across = (lax.rem(t + i, NT) for i in (3, 1, 2))

    def halves(first, rows):
        return pl.ds(first, rows // 2), pl.ds(first + rows // 2, rows // 2)

    def tensor_start(own, everyone, which, first=0, rows=ROWS):
        part = pl.ds(first, rows)
        for i, offset in ((0, 1), (1, 3)):
            copy = on_y(own.at[part], everyone.at[t, part], which, i, offset)
            copy.start()
            sends.append(copy)

    def tensor_forward(everyone, which, first=0, rows=ROWS):
        for i, offset, source in ((0, 1, before), (1, 3, after)):
            ref = everyone.at[source, pl.ds(first, rows)]
            on_y(ref, ref, which, i, offset).wait_recv()
            ref = everyone.at[source, halves(first, rows)[i]]
            copy = on_y(ref, ref, which, 2 + i, offset)
            copy.start()
            sends.append(copy)

    def tensor_end(everyone, which, first=0, rows=ROWS):
        for i, offset in ((0, 1), (1, 3)):
            ref = everyone.at[across, halves(first, rows)[i]]
            on_y(ref, ref, which, 2 + i, offset).wait_recv()

    def holder(source):
        return lax.rem(source, 2) == lax.div(z, 4)

    def piece(i):
        dest = 4 * lax.rem(t, 2) + i
        target = slab.at[lax.div(t, 2), z]
        source = up.at[:, pl.ds(i * 256, 256)]
        device = (place.d, xh * NZ + dest, t)
        return dest, source, remote(source, target, send_sem.at[0], a_rs.at[z], device)

    def spread_pieces():
        for i in range(4):
            dest, source, copy = piece(i)

            @pl.when(dest != z)
            def _(copy=copy):
                copy.start()

            @pl.when(dest == z)
            def _(source=source):
                slab[lax.div(t, 2), z] = source[...]

    def pieces_sent():
        for i in range(4):
            dest, _, copy = piece(i)

            @pl.when(dest != z)
            def _(copy=copy):
                copy.wait_send()

    def slab_half(source, i):
        return slab.at[lax.div(source, 2), pl.ds(4 * i, 4)]

    def share_start():
        @pl.when(holder(t))
        def _():
            for i in range(1, NZ):
                source = lax.rem(z + i, NZ)
                ref = slab.at[lax.div(t, 2), source]
                remote(ref, ref, send_sem.at[0], a_rs.at[source], place.zdev(1)).wait_recv()
            ref = slab.at[lax.div(t, 2)]
            on_y(ref, ref, 2, 0, 1).start()
            on_y(ref, ref, 2, 1, 3).start()

    def share_forward():
        @pl.when(holder(before))
        def _():
            for i, offset, source in ((0, 1, before), (1, 3, after)):
                ref = slab.at[lax.div(source, 2)]
                on_y(ref, ref, 2, i, offset).wait_recv()
                ref = slab_half(source, i)
                on_y(ref, ref, 2, 2 + i, offset).start()

    def share_end():
        @pl.when(holder(across))
        def _():
            for i, offset in ((0, 1), (1, 3)):
                ref = slab_half(across, i)
                on_y(ref, ref, 2, 2 + i, offset).wait_recv()

    def share_sent():
        @pl.when(holder(t))
        def _():
            ref = slab.at[lax.div(t, 2)]
            on_y(ref, ref, 2, 0, 1).wait_send()
            on_y(ref, ref, 2, 1, 3).wait_send()

        @pl.when(holder(before))
        def _():
            for i, offset, source in ((0, 1, before), (1, 3, after)):
                ref = slab_half(source, i)
                on_y(ref, ref, 2, 2 + i, offset).wait_send()

    stores = []

    def store(src, dst):
        copy = pltpu.make_async_copy(src, dst, store_sem.at[len(stores)])
        copy.start()
        stores.append(copy)

    def cross_start(term, sbuf, rbuf, which):
        value = term(across).astype(BF16)
        for i, offset in ((0, 1), (1, 3)):
            part = halves(0, ROWS)[i]
            sbuf[0, part] = value[i * half : (i + 1) * half]
            copy = on_y(sbuf.at[0, part], rbuf.at[0, part], which, 2 + i, offset)
            copy.start()
            sends.append(copy)

    def cross_forward(term, sbuf, rbuf, which):
        for i, offset, dest in ((0, 1, after), (1, 3, before)):
            value = term(dest)
            part = halves(0, ROWS)[i]
            ref = rbuf.at[0, part]
            on_y(ref, ref, which, 2 + i, offset).wait_recv()
            rest = slice((1 - i) * half, (2 - i) * half)
            sbuf[1 + i, part] = (value[i * half : (i + 1) * half] + ref[...]).astype(BF16)
            sbuf[1 + i, halves(0, ROWS)[1 - i]] = value[rest].astype(BF16)
            copy = on_y(sbuf.at[1 + i], rbuf.at[1 + i], which, i, offset)
            copy.start()
            sends.append(copy)

    def cross_end(own, rbuf, which, out):
        value = own[...]
        for i, offset in ((0, 1), (1, 3)):
            ref = rbuf.at[1 + i]
            on_y(ref, ref, which, i, offset).wait_recv()
            value = value + ref[...]
        out[...] = value.astype(BF16)

    load_tok.wait()
    tensor_start(tok, tok_all, 0)
    load_up.wait()
    spread_pieces()
    position = lax.broadcasted_iota(jnp.int32, (ROWS, HEAD_SIZE), 0) + place.s * ROWS
    angles = position.astype(F32) * freqs[...]
    cosine[...] = jnp.cos(angles)
    low = lax.broadcasted_iota(jnp.int32, (ROWS, HEAD_SIZE), 1) < HEAD_SIZE // 2
    sines = jnp.sin(angles)
    sine[...] = jnp.where(low, -sines, sines)
    groups = exponents.shape[1]
    group = lax.broadcasted_iota(jnp.int32, (ROWS, groups), 0) // SCALE_TOKENS
    group = group + place.s * (ROWS // SCALE_TOKENS)
    pick = lax.broadcasted_iota(jnp.int32, (ROWS, groups), 1) == group
    expo[...] = dot(pick.astype(F32).astype(BF16), exponents[...].astype(F32).astype(BF16), 1, 1)
    row = lax.broadcasted_iota(jnp.int32, (PAIR, HEAD_SIZE), 0)
    key_place[...] = jnp.where(row < ROWS, row, row + (NZ - 1) * ROWS)
    limit[...] = place.s * ROWS + lax.rem(
        lax.broadcasted_iota(jnp.int32, (1, QROWS), 1), jnp.int32(ROWS)
    )
    top[...] = jnp.full(top.shape, -jnp.inf, F32)
    total[...] = jnp.zeros(total.shape, F32)
    acc[...] = jnp.zeros(acc.shape, F32)
    dq[...] = jnp.zeros(dq.shape, F32)

    @pl.when(xh == 1)
    def _():
        dkv_other[...] = jnp.zeros(dkv_other.shape, BF16)

    def weight_rows(source):
        return pl.ds(pl.multiple_of(source * WIDTH, WIDTH), WIDTH)

    def project_kv(source):
        return dot(tok_all[source], wq[weight_rows(source), 512:768], 1, 0)

    def project_q(source):
        return dot(tok_all[source], wq[weight_rows(source), 0:512], 1, 0)

    def around(step):
        return lax.rem(z + step + NZ, NZ)

    def forward(zk):
        keys = kv[0, zk]
        values = kv[1, zk]
        for cut in range(0, QROWS, HEAD_SIZE):
            cut = slice(cut, cut + HEAD_SIZE)
            scores = dot(keys, q[cut], 1, 1)
            allowed = key_place[...] <= limit[:, cut] - zk * ROWS
            scores = jnp.where(allowed, scores, -jnp.inf)
            before = top[:, cut]
            now = jnp.maximum(before, jnp.max(scores, axis=0, keepdims=True))
            weights = jnp.exp2((scores - now) * SCALE2)
            alpha = jnp.exp2((before - now) * SCALE2)
            top[:, cut] = now
            total[:, cut] = total[:, cut] * alpha + jnp.sum(weights, axis=0, keepdims=True)
            acc[:, cut] = acc[:, cut] * alpha + dot(values, weights.astype(BF16), 0, 0)

    def merged_term(source):
        return dot(up_all[source], wo[:, weight_rows(source)], 1, 1)

    c, s = cosine[...], sine[...]

    def kv_part(column, i):
        def part(step, di, at):
            first = column * ROWS
            rows = pl.ds(pl.multiple_of(first, ROWS), ROWS)
            if step == 4:
                rows = pl.ds(pl.multiple_of(first + di * half, half), half)
            return kv.at[i, lax.rem(at + 2 * NZ, NZ), rows]

        return part

    own_rings = [gather_ring(place, kv_part(xh, i), i, send_sem, ag_rs, sends) for i in range(2)]
    other_rings = [
        gather_ring(place, kv_part(1 - xh, i), 2 + i, send_sem, ag_rs, sends, 2) for i in range(2)
    ]

    def step_kv(i):
        run(own_rings[i], 1)
        run(other_rings[i], 1)

    for load in loads:
        load.wait()
    projected = project_kv(t)
    tensor_forward(tok_all, 0)
    projected = projected + project_kv(before) + project_kv(after)
    tensor_end(tok_all, 0)
    tensor_start(up, up_all, 1)
    projected = projected + project_kv(across)
    rows = pl.ds(pl.multiple_of(xh * ROWS, ROWS), ROWS)
    kv[0, z, rows] = turn(projected[:, 0:128], c, s).astype(BF16)
    kv[1, z, rows] = projected[:, 128:256].astype(BF16)
    for i in range(2):
        own = kv.at[i, z, rows]
        run(own_rings[i], 1)
        for di, sign in ((0, 1), (1, -1)):
            copy = remote(
                own, own, send_sem.at[0], ag_rs.at[2 + i, di, 0], place.diagonal(sign)
            )
            copy.start()
            sends.append(copy)
        swap(own, own, (0, 14)[i])
    projected = project_q(t) + project_q(before) + project_q(after) + project_q(across)
    for h in range(QUERY_PER_KEY):
        q[pl.ds(h * ROWS, ROWS)] = turn(
            projected[:, h * HEAD_SIZE : (h + 1) * HEAD_SIZE], c, s
        ).astype(BF16)
    step_kv(0)
    step_kv(1)
    for i in range(2):
        other = kv_part(1 - xh, i)(1, 0, z)
        sem = (0, 14)[i]
        remote(other, other, send_sem.at[0], x_rs.at[sem], place.xdev()).wait_recv()
    x_tok = [swap(tok_all.at[2 * (1 - xh) + i], tok_other.at[i], 1 + i) for i in range(2)]
    forward(z)
    forward(around(1))
    step_kv(0)
    forward(around(-1))
    step_kv(1)
    forward(around(2))
    tensor_forward(up_all, 1)
    load_wo.wait()
    grad = merged_term(t) + merged_term(before)
    step_kv(0)
    forward(around(-2))
    step_kv(1)
    forward(around(3))
    grad = grad + merged_term(after)
    run(own_rings[0])
    run(other_rings[0])
    forward(around(-3))
    run(own_rings[1])
    run(other_rings[1])
    forward(around(4))

    out_t = (acc[...] / total[...]).astype(BF16)
    out = out_t.astype(F32).T.astype(BF16)
    for h in range(QUERY_PER_KEY):
        rows = out[h * ROWS : (h + 1) * ROWS]
        merged[:, h * HEAD_SIZE : (h + 1) * HEAD_SIZE] = rows
        merged_all[h // 2, z, :, (h % 2) * HEAD_SIZE : (h % 2 + 1) * HEAD_SIZE] = rows

    def merged_part(h):
        def part(step, di, at):
            ref = merged_all.at[h, lax.rem(at + 2 * NZ, NZ)]
            return ref.at[pl.ds(di * (ROWS // 2), ROWS // 2)] if step == 4 else ref

        return part

    merged_rings = [
        gather_ring(place, merged_part(h), h, send_sem, m_rs, sends) for h in range(2)
    ]

    def step_merged():
        for ring in merged_rings:
            run(ring, 1)

    step_merged()
    tensor_end(up_all, 1)
    grad = grad + merged_term(across)
    for h in range(QUERY_PER_KEY):
        do[pl.ds(h * ROWS, ROWS)] = grad[:, h * HEAD_SIZE : (h + 1) * HEAD_SIZE].astype(BF16)
    logsum[...] = top[...] * SCALE2 + jnp.log2(total[...])
    delta[...] = jnp.sum(do[...].astype(F32).T * out_t.astype(F32), axis=0, keepdims=True)

    def give_dkv(slot):
        return remote(
            dkv.at[slot, 0], dkv_other.at[slot], send_sem.at[0], x_rs.at[6 + slot], place.xdev()
        )

    def cross_dkv(slots):
        @pl.when(xh == 1)
        def _():
            for slot in slots:
                give_dkv(slot).start()

    def backward(slot, zk):
        keys = kv[0, zk]
        values = kv[1, zk]
        scores = dot(keys, q[...], 1, 1)
        allowed = key_place[:, 0:1] <= limit[...] - zk * ROWS
        probs = jnp.exp2(jnp.where(allowed, scores * SCALE2 - logsum[...], -jnp.inf))
        grad_probs = dot(values, do[...], 1, 1)
        grad_scores = (probs * (grad_probs - delta[...])).astype(BF16)
        dv = dot(probs.astype(BF16), do[...], 1, 0).astype(BF16)
        dk = (dot(grad_scores, q[...], 1, 0) * SCALE).astype(BF16)
        dq[...] += dot(keys, grad_scores, 0, 0)
        for column in range(2):
            rows = slice(column * ROWS, (column + 1) * ROWS)
            dkv[slot, column, 0:ROWS] = dk[rows]
            dkv[slot, column, ROWS:PAIR] = dv[rows]

    kv_here = set()

    def kv_term(step, di):
        slot = {4: 0, 3: 1, 2: 3, 1: 5, 0: 7}[step] + (di if step in (1, 2, 3) else 0)
        if slot not in kv_here:
            kv_here.add(slot)

            @pl.when(xh == 0)
            def _():
                give_dkv(slot).wait_recv()

        return dkv[slot, xh].astype(F32) + dkv_other[slot].astype(F32)

    ring_kv = TwoStages(place, PAIR, kv_term, kv_sb, kv_rb, send_sem, kv_rs, sends)

    def attended_term(dest):
        return dot(merged[...], wo[:, pl.ds(pl.multiple_of(dest * WIDTH, WIDTH), WIDTH)], 1, 0)

    def columns(dest):
        return pl.ds(pl.multiple_of(lax.rem(dest, 4) * 256, 256), 256)

    def load_q(dest, sub, part, step, di, width=256, first=0):
        shard = lax.div(dest, 4)
        left = tok_all[2 * xh + shard, :, columns(dest)]
        left_other = tok_other[shard, :, columns(dest)]
        if part is not None:
            left = left[:, part * 128 : (part + 1) * 128]
            left_other = left_other[:, part * 128 : (part + 1) * 128]
        cut = slice(first + sub * width, first + (sub + 1) * width)
        return dot(left, gqkv[0, :, cut], 0, 0) + dot(left_other, gqkv[1, :, cut], 0, 0)

    def done_q(sub, value):
        cut = pl.ds(sub * 256, 256)
        gwq[sub] = value.astype(BF16)
        store(gwq.at[sub], gwq_hbm.at[:, cut])

    ring_q = scatter_ring(place, (0, 1), 256, load_q, q_sb, q_rb, send_sem, q_rs, sends, done_q)

    def load_k(dest, sub, part, step, di):
        return load_q(dest, sub, part, step, di, 128, 512)

    def done_k(sub, value):
        cut = pl.ds(sub * 128, 128)
        gwq[2, :, cut] = value.astype(BF16)
        store(gwq.at[2, :, cut], gwq_hbm.at[:, pl.ds(512 + sub * 128, 128)])

    ring_k = scatter_ring(place, (0, 1), 256, load_k, k_sb, k_rb, send_sem, k_rs, sends, done_k)

    def squeeze(value, column):
        e = expo[:, column : column + 1]
        sent = jnp.clip(value * jnp.exp2(-e), -127.0, 127.0).astype(BF16)
        return sent.astype(F32) * jnp.exp2(e)

    share_start()
    backward(0, around(4))
    backward(1, around(3))
    backward(2, around(-3))
    cross_dkv((0, 1, 2))
    backward(3, around(2))
    backward(4, around(-2))
    step_merged()
    backward(5, around(1))
    backward(6, around(-1))
    backward(7, z)
    grad = dq[...].T * SCALE
    x_gq = []
    for h in range(QUERY_PER_KEY):
        gqkv[0, :, h * HEAD_SIZE : (h + 1) * HEAD_SIZE] = turn(
            squeeze(grad[h * ROWS : (h + 1) * ROWS], h), c, -s
        ).astype(BF16)
        if h % 2:
            cut = pl.ds((h - 1) * HEAD_SIZE, 2 * HEAD_SIZE)
            sem = (4, 15)[h // 2]
            x_gq.append(swap(gqkv.at[0, :, cut], gqkv.at[1, :, cut], sem))
    cross_dkv((3, 4, 5, 6, 7))
    step_merged()
    ring_kv.far()
    cross_start(attended_term, att_s, att_r, 3)
    for copy in x_tok:
        copy.wait_recv()
    x_gq[0].wait_recv()
    run(ring_q, 1)
    x_gq[1].wait_recv()
    run(ring_q, 1)
    step_merged()
    ring_kv.middle()
    ring_kv.near()
    share_forward()
    run(ring_q, 2)
    kv_sum = ring_kv.end()
    gqkv[0, :, 512:640] = turn(squeeze(kv_sum[:ROWS], 4), c, -s).astype(BF16)
    gqkv[0, :, 640:768] = squeeze(kv_sum[ROWS:], 5).astype(BF16)
    x_gkv = swap(gqkv.at[0, :, pl.ds(512, 256)], gqkv.at[1, :, pl.ds(512, 256)], 5)

    def tokens_term(dest):
        return dot(gqkv[0], wq[pl.ds(pl.multiple_of(dest * WIDTH, WIDTH), WIDTH)], 1, 1)

    cross_forward(attended_term, att_s, att_r, 3)
    cross_start(tokens_term, tok_s, tok_r, 4)
    run(ring_q, 2)
    x_gkv.wait_recv()
    run(ring_k, 2)
    for ring in merged_rings:
        run(ring)
    share_end()

    def out_term(h, column):
        tokens = NZ * ROWS
        return dot(
            merged_all[h].reshape(tokens, 256), slab[column].reshape(tokens, 256), 0, 0
        )

    for h in range(2):
        o_sb[pl.ds(h * 256, 256)] = out_term(h, 1 - xh).astype(BF16)
    x_o = swap(o_sb, o_rb, 3)
    att_own[...] = attended_term(t)
    tok_own[...] = tokens_term(t)
    run(ring_k, 2)
    run(ring_q, 2)
    run(ring_k, 2)
    cross_forward(tokens_term, tok_s, tok_r, 4)
    cross_end(att_own, att_r, 3, attended)
    store(attended, attended_hbm)
    run(ring_q)
    run(ring_k, 2)
    x_o.wait_recv()
    for h in range(2):
        rows = pl.ds(h * 256, 256)
        gwo[rows] = (out_term(h, xh) + o_rb[rows]).astype(BF16)
    store(gwo, gwo_hbm)
    cross_end(tok_own, tok_r, 4, grad_tokens)
    store(grad_tokens, grad_tokens_hbm)
    run(ring_k)
    pieces_sent()

    @pl.when(xh == 1)
    def _():
        for slot in range(NZ):
            give_dkv(slot).wait_send()

    share_sent()
    for copy in sends:
        copy.wait_send()
    for copy in stores:
        copy.wait()


def layer(tok, up, wq, wo, freqs, exponents):
    vmem = pl.BlockSpec(memory_space=pltpu.VMEM)
    hbm = pl.BlockSpec(memory_space=pl.ANY)
    shape = jax.ShapeDtypeStruct
    dma = pltpu.SemaphoreType.DMA
    buf = pltpu.VMEM
    heads = QUERY_PER_KEY * HEAD_SIZE
    return pl.pallas_call(
        layer_kernel,
        name="layer",
        out_shape=[
            shape((ROWS, WIDTH), BF16),
            shape((ROWS, WIDTH), BF16),
            shape((256, 768), BF16),
            shape((512, 256), BF16),
        ],
        in_specs=[hbm, hbm, hbm, hbm, vmem, vmem],
        out_specs=[hbm] * 4,
        scratch_shapes=[
            buf(wq.shape, BF16),
            buf(wo.shape, BF16),
            buf((NT, ROWS, WIDTH), BF16),
            buf((NT, ROWS, WIDTH), BF16),
            buf((2, ROWS, WIDTH), BF16),
            buf((2, NZ, ROWS, 256), BF16),
            buf((ROWS, HEAD_SIZE), F32),
            buf((ROWS, HEAD_SIZE), F32),
            buf((ROWS, 6), F32),
            buf((QROWS, HEAD_SIZE), BF16),
            buf((2, NZ, PAIR, HEAD_SIZE), BF16),
            buf((QROWS, HEAD_SIZE), BF16),
            buf((ROWS, heads), BF16),
            buf((2, NZ, ROWS, 256), BF16),
            buf((2, ROWS, 768), BF16),
            buf((PAIR, HEAD_SIZE), jnp.int32),
            buf((1, QROWS), jnp.int32),
            buf((1, QROWS), F32),
            buf((1, QROWS), F32),
            buf((HEAD_SIZE, QROWS), F32),
            buf((1, QROWS), F32),
            buf((1, QROWS), F32),
            buf((HEAD_SIZE, QROWS), F32),
            buf((NZ, 2, PAIR, HEAD_SIZE), BF16),
            buf((NZ, PAIR, HEAD_SIZE), BF16),
            buf((ROWS, WIDTH), F32),
            buf((3, ROWS, WIDTH), BF16),
            buf((3, ROWS, WIDTH), BF16),
            buf((ROWS, WIDTH), F32),
            buf((3, ROWS, WIDTH), BF16),
            buf((3, ROWS, WIDTH), BF16),
            buf((2, 4, PAIR, HEAD_SIZE), BF16),
            buf((2, 4, PAIR, HEAD_SIZE), BF16),
            buf((512, 256), BF16),
            buf((512, 256), BF16),
            buf((2, 4, 2, 256, 256), BF16),
            buf((2, 4, 2, 256, 256), BF16),
            buf((2, 4, 2, 256, 128), BF16),
            buf((2, 4, 2, 256, 128), BF16),
            buf((ROWS, WIDTH), BF16),
            buf((ROWS, WIDTH), BF16),
            buf((3, 256, 256), BF16),
            buf((512, 256), BF16),
            dma((7,)),
            dma((7,)),
            dma((1,)),
            dma((5, 4)),
            dma((16,)),
            dma((4, 2, 4)),
            dma((2, 4)),
            dma((2, 2, 4)),
            dma((NZ,)),
            dma((2, 4, 2)),
            dma((2, 4, 2)),
        ],
        compiler_params=pltpu.CompilerParams(
            collective_id=0, has_side_effects=True, vmem_limit_bytes=VMEM_LIMIT
        ),
    )(tok, up, wq, wo, freqs, exponents)


def settle_kernel(*refs):
    number = (len(refs) - 1) // 3
    sources, targets, held, sems = (
        refs[:number],
        refs[number : 2 * number],
        refs[2 * number : 3 * number],
        refs[-1],
    )
    for i in range(number):
        pltpu.make_async_copy(sources[i], held[i], sems.at[0, i]).start()
    for i in range(number):
        pltpu.make_async_copy(sources[i], held[i], sems.at[0, i]).wait()
        pltpu.make_async_copy(held[i], targets[i], sems.at[1, i]).start()
    for i in range(number):
        pltpu.make_async_copy(held[i], targets[i], sems.at[1, i]).wait()


def settle(*arrays):
    hbm = pl.BlockSpec(memory_space=pl.ANY)
    return pl.pallas_call(
        settle_kernel,
        name="settle",
        out_shape=[jax.ShapeDtypeStruct(a.shape, a.dtype) for a in arrays],
        in_specs=[hbm] * len(arrays),
        out_specs=[hbm] * len(arrays),
        scratch_shapes=[pltpu.VMEM(a.shape, a.dtype) for a in arrays]
        + [pltpu.SemaphoreType.DMA((2, len(arrays)))],
        compiler_params=pltpu.CompilerParams(vmem_limit_bytes=VMEM_LIMIT),
    )(*arrays)


def local(tokens, input_projection_weight, w_out, upstream, exponents):
    half = HEAD_SIZE // 2
    freqs = np.power(np.float32(THETA), -np.arange(half, dtype=np.float32) * 2.0 / HEAD_SIZE)
    freqs = jnp.asarray(np.tile(freqs, 2).reshape(1, HEAD_SIZE), F32)
    return settle(
        *layer(tokens, upstream, input_projection_weight, w_out, freqs, exponents.T)
    )


def solution(mesh):
    in_specs = (
        P(("dp", "seq"), "tensor"),
        P(None, "tensor"),
        P("tensor", None),
        P(("dp", "seq"), "tensor"),
        P("dp", "tensor"),
    )
    out_specs = (
        P(("dp", "seq"), "tensor"),
        P(("dp", "seq"), "tensor"),
        P(("dp", "seq"), "tensor"),
        P(("dp", "tensor"), "seq"),
    )
    return jax.shard_map(local, mesh=mesh, in_specs=in_specs, out_specs=out_specs, check_vma=False)
```

time: 120 us -> 112 us (0.933); the launches traced: 118 us -> 112 us
  Pallas kernels: 117 us -> 111 us
    pallas_call x1, Pallas kernels: 115 us -> 109 us  [layer(): pl.pallas_call(layer_kernel, name='layer', out_shape=[shape((ROWS, WIDTH)...]
where the time goes in v4:
time: 112 us
  Pallas kernels  111 us (99%)
    pallas_call x1, Pallas kernels, layer(): pl.pallas_call(layer_kernel, name='layer', out_shape=[shape((ROWS, WIDTH)...  109 us

profile of v4, /device:TPU:2, one launch (start us, length us, event | category | flops | bytes accessed | tf_op | source)
XLA Modules:
  0.0 111.5 jit_solution(14302586678111591194)
XLA Ops:
  0.6 108.6 %layer.1 = (bf16[192,1024]{1,0:T(8,128)(2,1)}, bf16[192,1024]{1,0:T(8,128)(2,1)}, bf16[256,768]{1,0:T(8,128)(2,1)}, bf16[512,256]{1,0:T(8,128)(2,1)}) custom-call(bf16[192,1024]{1,0:T(8,128)(2,1)} %tok_hbm.1, bf16[192,1024]{1,0:T(8,128)(2,1)} %up_hbm.1, bf16[4096,768]{1,0:T(8,128)(2,1)} %wq_hbm.1, bf16[512,4096]{1,0:T(8,128)(2,1)} %wo_hbm.1, ...), custom_call_target="tpu_custom_call" | custom-call | tf_op jit(solution)/shard_map/layer/pallas_call | solution.py:736
  109.2 2.2 %settle.1 = (bf16[192,1024]{1,0:T(8,128)(2,1)}, bf16[192,1024]{1,0:T(8,128)(2,1)}, bf16[256,768]{1,0:T(8,128)(2,1)}, bf16[512,256]{1,0:T(8,128)(2,1)}) custom-call(bf16[192,1024]{1,0:T(8,128)(2,1)} %get-tuple-element.8.refs_0_, bf16[192,1024]{1,0:T(8,128)(2,1)} %get-tuple-element.9.refs_1_, bf16[256,768]{1,0:T(8,128)(2,1)} %get-tuple-element.10.refs_2_, ...), custom_call_target="tpu_custom_call" | custom-call | tf_op jit(solution)/shard_map/settle/pallas_call | solution.py:828

commit v5 on v4

--- a/solution.py
+++ b/solution.py
@@ -56,7 +56,7 @@
 
     def enter(self):
         barrier = pltpu.get_barrier_semaphore()
-        partners = [self.tensor(1), self.tensor(2), self.tensor(3)]
+        partners = [self.tensor(1), self.tensor(3)]
         partners += [self.zdev(i) for i in range(1, NZ)] + [self.xdev()]
         partners += [self.diagonal(1), self.diagonal(-1)]
         for partner in partners:
@@ -256,25 +256,30 @@
     def halves(first, rows):
         return pl.ds(first, rows // 2), pl.ds(first + rows // 2, rows // 2)
 
-    def tensor_start(own, everyone, which, first=0, rows=ROWS):
-        part = pl.ds(first, rows)
-        for i, offset in ((0, 1), (1, 3)):
-            copy = on_y(own.at[part], everyone.at[t, part], which, i, offset)
-            copy.start()
-            sends.append(copy)
-
-    def tensor_forward(everyone, which, first=0, rows=ROWS):
+    def tensor_start(everyone, which):
+        for rest in range(2):
+            for i, offset in ((0, 1), (1, 3)):
+                ref = everyone.at[t, halves(0, ROWS)[(i + rest) % 2]]
+                copy = on_y(ref, ref, which, i + 4 * rest, offset)
+                copy.start()
+                sends.append(copy)
+
+    def tensor_forward(everyone, which):
         for i, offset, source in ((0, 1, before), (1, 3, after)):
-            ref = everyone.at[source, pl.ds(first, rows)]
+            ref = everyone.at[source, halves(0, ROWS)[i]]
             on_y(ref, ref, which, i, offset).wait_recv()
-            ref = everyone.at[source, halves(first, rows)[i]]
             copy = on_y(ref, ref, which, 2 + i, offset)
             copy.start()
             sends.append(copy)
 
-    def tensor_end(everyone, which, first=0, rows=ROWS):
+    def tensor_rest(everyone, which):
+        for i, offset, source in ((0, 1, before), (1, 3, after)):
+            ref = everyone.at[source, halves(0, ROWS)[1 - i]]
+            on_y(ref, ref, which, 4 + i, offset).wait_recv()
+
+    def tensor_end(everyone, which):
         for i, offset in ((0, 1), (1, 3)):
-            ref = everyone.at[across, halves(first, rows)[i]]
+            ref = everyone.at[across, halves(0, ROWS)[i]]
             on_y(ref, ref, which, 2 + i, offset).wait_recv()
 
     def holder(source):
@@ -388,7 +393,7 @@
         out[...] = value.astype(BF16)
 
     load_tok.wait()
-    tensor_start(tok, tok_all, 0)
+    tensor_start(tok_all, 0)
     load_up.wait()
     spread_pieces()
     position = lax.broadcasted_iota(jnp.int32, (ROWS, HEAD_SIZE), 0) + place.s * ROWS
@@ -472,9 +477,10 @@
         load.wait()
     projected = project_kv(t)
     tensor_forward(tok_all, 0)
+    tensor_rest(tok_all, 0)
     projected = projected + project_kv(before) + project_kv(after)
     tensor_end(tok_all, 0)
-    tensor_start(up, up_all, 1)
+    tensor_start(up_all, 1)
     projected = projected + project_kv(across)
     rows = pl.ds(pl.multiple_of(xh * ROWS, ROWS), ROWS)
     kv[0, z, rows] = turn(projected[:, 0:128], c, s).astype(BF16)
@@ -508,6 +514,7 @@
     step_kv(1)
     forward(around(2))
     tensor_forward(up_all, 1)
+    tensor_rest(up_all, 1)
     load_wo.wait()
     grad = merged_term(t) + merged_term(before)
     step_kv(0)
@@ -540,11 +547,11 @@
         gather_ring(place, merged_part(h), h, send_sem, m_rs, sends) for h in range(2)
     ]
 
-    def step_merged():
-        for ring in merged_rings:
-            run(ring, 1)
-
-    step_merged()
+    def step_merged(h):
+        run(merged_rings[h], 1)
+
+    step_merged(0)
+    step_merged(1)
     tensor_end(up_all, 1)
     grad = grad + merged_term(across)
     for h in range(QUERY_PER_KEY):
@@ -557,11 +564,10 @@
             dkv.at[slot, 0], dkv_other.at[slot], send_sem.at[0], x_rs.at[6 + slot], place.xdev()
         )
 
-    def cross_dkv(slots):
+    def cross_dkv(slot):
         @pl.when(xh == 1)
         def _():
-            for slot in slots:
-                give_dkv(slot).start()
+            give_dkv(slot).start()
 
     def backward(slot, zk):
         keys = kv[0, zk]
@@ -578,6 +584,7 @@
             rows = slice(column * ROWS, (column + 1) * ROWS)
             dkv[slot, column, 0:ROWS] = dk[rows]
             dkv[slot, column, ROWS:PAIR] = dv[rows]
+        cross_dkv(slot)
 
     kv_here = set()
 
@@ -636,11 +643,11 @@
     backward(0, around(4))
     backward(1, around(3))
     backward(2, around(-3))
-    cross_dkv((0, 1, 2))
     backward(3, around(2))
+    step_merged(0)
     backward(4, around(-2))
-    step_merged()
     backward(5, around(1))
+    step_merged(1)
     backward(6, around(-1))
     backward(7, z)
     grad = dq[...].T * SCALE
@@ -653,21 +660,22 @@
             cut = pl.ds((h - 1) * HEAD_SIZE, 2 * HEAD_SIZE)
             sem = (4, 15)[h // 2]
             x_gq.append(swap(gqkv.at[0, :, cut], gqkv.at[1, :, cut], sem))
-    cross_dkv((3, 4, 5, 6, 7))
-    step_merged()
+    step_merged(0)
     ring_kv.far()
+    step_merged(1)
     cross_start(attended_term, att_s, att_r, 3)
+    ring_kv.middle()
+    step_merged(0)
+    step_merged(1)
+    ring_kv.near()
     for copy in x_tok:
         copy.wait_recv()
+    share_forward()
+    cross_forward(attended_term, att_s, att_r, 3)
     x_gq[0].wait_recv()
     run(ring_q, 1)
     x_gq[1].wait_recv()
     run(ring_q, 1)
-    step_merged()
-    ring_kv.middle()
-    ring_kv.near()
-    share_forward()
-    run(ring_q, 2)
     kv_sum = ring_kv.end()
     gqkv[0, :, 512:640] = turn(squeeze(kv_sum[:ROWS], 4), c, -s).astype(BF16)
     gqkv[0, :, 640:768] = squeeze(kv_sum[ROWS:], 5).astype(BF16)
@@ -676,8 +684,8 @@
     def tokens_term(dest):
         return dot(gqkv[0], wq[pl.ds(pl.multiple_of(dest * WIDTH, WIDTH), WIDTH)], 1, 1)
 
-    cross_forward(attended_term, att_s, att_r, 3)
     cross_start(tokens_term, tok_s, tok_r, 4)
+    att_own[...] = attended_term(t)
     run(ring_q, 2)
     x_gkv.wait_recv()
     run(ring_k, 2)
@@ -694,16 +702,16 @@
     for h in range(2):
         o_sb[pl.ds(h * 256, 256)] = out_term(h, 1 - xh).astype(BF16)
     x_o = swap(o_sb, o_rb, 3)
-    att_own[...] = attended_term(t)
     tok_own[...] = tokens_term(t)
-    run(ring_k, 2)
     run(ring_q, 2)
     run(ring_k, 2)
     cross_forward(tokens_term, tok_s, tok_r, 4)
+    run(ring_k, 2)
+    run(ring_q, 2)
     cross_end(att_own, att_r, 3, attended)
     store(attended, attended_hbm)
+    run(ring_k, 2)
     run(ring_q)
-    run(ring_k, 2)
     x_o.wait_recv()
     for h in range(2):
         rows = pl.ds(h * 256, 256)
@@ -791,7 +799,7 @@
             dma((7,)),
             dma((7,)),
             dma((1,)),
-            dma((5, 4)),
+            dma((5, 6)),
             dma((16,)),
             dma((4, 2, 4)),
             dma((2, 4)),

time: 112 us -> 110 us (0.982)
  Pallas kernels: 111 us -> 108 us
    pallas_call x1, Pallas kernels: 109 us -> 106 us  [layer(): pl.pallas_call(layer_kernel, name='layer', out_shape=[shape((ROWS, WIDTH)...]
where the time goes in v5:
time: 110 us; the launch traced here: 109 us
  Pallas kernels  108 us (98%)
    pallas_call x1, Pallas kernels, layer(): pl.pallas_call(layer_kernel, name='layer', out_shape=[shape((ROWS, WIDTH)...  106 us

profile of v5, /device:TPU:2, one launch (start us, length us, event | category | flops | bytes accessed | tf_op | source)
XLA Modules:
  0.0 108.9 jit_solution(17401503967159223061)
XLA Ops:
  0.6 105.9 %layer.1 = (bf16[192,1024]{1,0:T(8,128)(2,1)}, bf16[192,1024]{1,0:T(8,128)(2,1)}, bf16[256,768]{1,0:T(8,128)(2,1)}, bf16[512,256]{1,0:T(8,128)(2,1)}) custom-call(bf16[192,1024]{1,0:T(8,128)(2,1)} %tok_hbm.1, bf16[192,1024]{1,0:T(8,128)(2,1)} %up_hbm.1, bf16[4096,768]{1,0:T(8,128)(2,1)} %wq_hbm.1, bf16[512,4096]{1,0:T(8,128)(2,1)} %wo_hbm.1, ...), custom_call_target="tpu_custom_call" | custom-call | tf_op jit(solution)/shard_map/layer/pallas_call | solution.py:744
  106.6 2.2 %settle.1 = (bf16[192,1024]{1,0:T(8,128)(2,1)}, bf16[192,1024]{1,0:T(8,128)(2,1)}, bf16[256,768]{1,0:T(8,128)(2,1)}, bf16[512,256]{1,0:T(8,128)(2,1)}) custom-call(bf16[192,1024]{1,0:T(8,128)(2,1)} %get-tuple-element.8.refs_0_, bf16[192,1024]{1,0:T(8,128)(2,1)} %get-tuple-element.9.refs_1_, bf16[256,768]{1,0:T(8,128)(2,1)} %get-tuple-element.10.refs_2_, ...), custom_call_target="tpu_custom_call" | custom-call | tf_op jit(solution)/shard_map/settle/pallas_call | solution.py:836

commit v6 on v5

--- a/solution.py
+++ b/solution.py
@@ -500,13 +500,13 @@
         q[pl.ds(h * ROWS, ROWS)] = turn(
             projected[:, h * HEAD_SIZE : (h + 1) * HEAD_SIZE], c, s
         ).astype(BF16)
+    x_tok = [swap(tok_all.at[2 * (1 - xh) + i], tok_other.at[i], 1 + i) for i in range(2)]
     step_kv(0)
     step_kv(1)
     for i in range(2):
         other = kv_part(1 - xh, i)(1, 0, z)
         sem = (0, 14)[i]
         remote(other, other, send_sem.at[0], x_rs.at[sem], place.xdev()).wait_recv()
-    x_tok = [swap(tok_all.at[2 * (1 - xh) + i], tok_other.at[i], 1 + i) for i in range(2)]
     forward(z)
     forward(around(1))
     step_kv(0)

time: 110 us -> 109 us (level)
  no operation moved by 1% of the time
where the time goes in v6:
time: 109 us
  Pallas kernels  108 us (99%)
    pallas_call x1, Pallas kernels, layer(): pl.pallas_call(layer_kernel, name='layer', out_shape=[shape((ROWS, WIDTH)...  106 us

profile of v6, /device:TPU:2, one launch (start us, length us, event | category | flops | bytes accessed | tf_op | source)
XLA Modules:
  0.0 108.7 jit_solution(6857469273949956973)
XLA Ops:
  0.6 105.8 %layer.1 = (bf16[192,1024]{1,0:T(8,128)(2,1)}, bf16[192,1024]{1,0:T(8,128)(2,1)}, bf16[256,768]{1,0:T(8,128)(2,1)}, bf16[512,256]{1,0:T(8,128)(2,1)}) custom-call(bf16[192,1024]{1,0:T(8,128)(2,1)} %tok_hbm.1, bf16[192,1024]{1,0:T(8,128)(2,1)} %up_hbm.1, bf16[4096,768]{1,0:T(8,128)(2,1)} %wq_hbm.1, bf16[512,4096]{1,0:T(8,128)(2,1)} %wo_hbm.1, ...), custom_call_target="tpu_custom_call" | custom-call | tf_op jit(solution)/shard_map/layer/pallas_call | solution.py:744
  106.4 2.2 %settle.1 = (bf16[192,1024]{1,0:T(8,128)(2,1)}, bf16[192,1024]{1,0:T(8,128)(2,1)}, bf16[256,768]{1,0:T(8,128)(2,1)}, bf16[512,256]{1,0:T(8,128)(2,1)}) custom-call(bf16[192,1024]{1,0:T(8,128)(2,1)} %get-tuple-element.8.refs_0_, bf16[192,1024]{1,0:T(8,128)(2,1)} %get-tuple-element.9.refs_1_, bf16[256,768]{1,0:T(8,128)(2,1)} %get-tuple-element.10.refs_2_, ...), custom_call_target="tpu_custom_call" | custom-call | tf_op jit(solution)/shard_map/settle/pallas_call | solution.py:836
